TPU v7x, 32 devices: a whole 2x2x4 slice. The times are simulated.
32 devices in a mesh: dp: 8 (over z, x), mp: 4 (over y, core).
Axes of the slice: x: 2, y: 2, z: 4, core: 2. Of those that a mesh axis runs over, the one named last changes fastest.
Arguments:
- tokens: bfloat16 [32768, 768], P(('dp', 'mp')), may hold values from -6 to 6
- lengths: int32 [128], P('dp'), may hold values from 65 to 512, as said below
- cotangent: bfloat16 [32768, 768], P(('dp', 'mp')), may hold values from -6 to 6
- w_qkv: float32 [768, 12, 192], P('dp', 'mp'), may hold values from -0.109375 to 0.109375
- w_o: float32 [768, 768], P(('dp', 'mp')), may hold values from -0.875 to 0.875
- w_in: float32 [768, 3072], P(None, ('dp', 'mp')), may hold values from -0.21875 to 0.21875
- w_out: float32 [3072, 768], P(('dp', 'mp')), may hold values from -0.109375 to 0.109375
- gain_attn: float32 [768], replicated, may hold values from 0.5 to 1.5
- gain_ffn: float32 [768], replicated, may hold values from 0.5 to 1.5
- pos_table: float32 [32, 12], replicated, may hold values from -4 to 4
- phm_rules: float32 [4, 4, 4], replicated, may hold values from -4 to 4
- down_left: float32 [4, 192], replicated, may hold values from -1.2 to 1.2
- down_right: float32 [4, 12], replicated, may hold values from -1.2 to 1.2
- up_left: float32 [4, 12], replicated, may hold values from -1.2 to 1.2
- up_right: float32 [4, 192], replicated, may hold values from -1.2 to 1.2
Outputs:
- out: bfloat16 [32768, 768], P(('dp', 'mp'))
- grad_tokens: bfloat16 [32768, 768], P(('dp', 'mp'))
- grad_w_qkv: float32 [768, 12, 192], P('dp', 'mp')
- grad_w_o: float32 [768, 768], P(('dp', 'mp'))
- grad_w_in: float32 [768, 3072], P(None, ('dp', 'mp'))
- grad_w_out: float32 [3072, 768], P(('dp', 'mp'))
- grad_gain_attn: float32 [768], replicated
- grad_gain_ffn: float32 [768], replicated
- grad_pos_table: float32 [32, 12], replicated
- grad_phm_rules: float32 [4, 4, 4], replicated
- grad_down_left: float32 [4, 192], replicated
- grad_down_right: float32 [4, 12], replicated
- grad_up_left: float32 [4, 12], replicated
- grad_up_right: float32 [4, 192], replicated
Inputs may be any that keep to these rules, and one draw needn't show every extreme that they name: `lengths`: entry g * 16 + j is the length of sequence j of group g; its slot length is 512 for j below 4, 256 for j below 8, else 128; each length is more than half of its slot length and at most the slot length, and in every group one of the first 4 sequences fills its slot.
All inputs are finite; a program needn't handle non-finite values.
Results may differ from a plain program's by a relative error of at most 0.024.
The roundings to bfloat16 on the way count: a program that leaves them out, or rounds other values in their place, can miss the bound.
Values may be sent and summed in bfloat16 or wider, within the bound.
A program may use at most 192 MiB of HBM per device.

v0:
```python
import functools
import itertools

import jax
import jax.experimental.pallas as pl
import jax.experimental.pallas.tpu as pltpu
import jax.numpy as jnp
import numpy as np
from jax import lax
from jax.sharding import PartitionSpec as P

D = 768
DH = 64
NB = 32
MAXDIST = 128
ADAPT = 48
KRON = 4
LEN_LONG = 512
LEN_MID = 256
LEN_SHORT = 128
SEG = 128


NORM_EPS = 1e-06
FULL_PRECISION = lax.Precision.HIGHEST


def rel_buckets(length):
    offsets = np.arange(-(length - 1), length)
    half_count = NB // 2
    exact_count = half_count // 2
    upward = (offsets > 0).astype(np.int64) * half_count
    distance = np.abs(offsets)
    scaled = (
        np.log(np.maximum(distance, 1) / exact_count)
        / np.log(MAXDIST / exact_count)
        * (half_count - exact_count)
    )
    far_bucket = np.minimum(
        exact_count + np.floor(np.maximum(scaled, 0.0)).astype(np.int64), half_count - 1
    )
    return upward + np.where(distance < exact_count, distance, far_bucket)


def normed(values, gain):
    return values * lax.rsqrt(jnp.mean(values * values, axis=-1, keepdims=True) + NORM_EPS) * gain


MESH = pl.DeviceIdType.MESH


class Place:
    def __init__(self, depth):
        d, m = lax.axis_index("dp"), lax.axis_index("mp")
        self.depth = depth
        self.d, self.m = d, m
        self.z, self.x, self.y, self.c = d // 2, d % 2, m // 2, m % 2
        dx, dy, c = 1 - 2 * self.x, 2 - 4 * self.y, self.c
        self.sib = (d, m + 1 - 2 * c)
        self.right, self.left = (d + 2, m), (d - 2, m)
        self.mp_peer = ((d, m + 1 - 2 * c), (d, m + dy), (d, 3 - m))
        self.xn, self.yn = (d + dx, m), (d, m + dy)
        self.a_nbr = (d + (1 - c) * dx, m + c * dy)
        self.b_nbr = (d + c * dx, m + (1 - c) * dy)
        self.a = self.x + c * (self.y - self.x)
        self.b = self.y + c * (self.x - self.y)

    def by_core(self, run):
        for core in (0, 1):
            pl.when(self.c == core)(functools.partial(run, core))

    def order(self, k):
        n = self.depth
        base = k // 2 if k % 2 == 0 else n - 1 - k // 2
        near = 1 - jnp.minimum(self.z // max(n // 2, 1), 1)
        return base + near * (n - 1 - 2 * base)

    def nearest(self, e):
        n, z = self.depth, self.z
        ahead = 1 - 2 * (z // ((n + 1) // 2))
        short = jnp.minimum(z, n - 1 - z)
        around = (1 - 2 * (e % 2)) * ((e + 1) // 2)
        return z + ahead * jnp.where(e <= 2 * short, around, e - short)

    def flip(self, bit):
        step = 1 << bit
        return (self.d + step * (1 - 2 * ((self.d // step) % 2)), self.m)

    def barrier(self, bits):
        self.greet(bits)
        self.meet(bits)

    def pals(self, bits):
        return [*self.mp_peer, self.xn] + [self.flip(bit) for bit in range(2, bits)]

    def greet(self, bits):
        sem = pltpu.get_barrier_semaphore()

        def greet(dev):
            pl.semaphore_signal(sem, 1, device_id=dev, device_id_type=MESH)

        for dev in self.pals(bits):
            greet(dev)
        pl.when(self.z > 0)(lambda: greet(self.left))
        pl.when(self.z < self.depth - 1)(lambda: greet(self.right))

    def meet(self, bits):
        ends = jnp.minimum(self.z, 1) + jnp.minimum(self.depth - 1 - self.z, 1)
        pl.semaphore_wait(pltpu.get_barrier_semaphore(), len(self.pals(bits)) + ends)


def remote(src, dst, send, recv, dev):
    return pltpu.make_async_remote_copy(
        src_ref=src, dst_ref=dst, send_sem=send, recv_sem=recv, device_id=dev, device_id_type=MESH
    )


def slot_of(buf, by_head, p):
    return buf.at[p.y, p.c, p.z, p.x] if by_head else buf.at[p.z, p.x, p.y, p.c]


def pair_of(buf, by_head, core, b, z):
    if by_head:
        return buf.at[b, 0, z] if core == 0 else buf.at[:, 1, z, b]
    return buf.at[z, :, b, 0] if core == 0 else buf.at[z, b, :, 1]


class Gather:
    def __init__(self, p, by_head, shard, buf, send, recv, own):
        self.p, self.by_head, self.shard, self.buf = p, by_head, shard, buf
        self.send, self.recv, self.own = send, recv, own
        n = p.depth
        self.first = remote(shard, slot_of(buf, by_head, p), send.at[5 * n], recv.at[4 * n], p.a_nbr)
        self.keep = pltpu.make_async_copy(shard, slot_of(buf, by_head, p), own)

    @staticmethod
    def sems(n):
        return [
            pltpu.SemaphoreType.DMA((5 * n + 1,)),
            pltpu.SemaphoreType.DMA((4 * n + 1,)),
            pltpu.SemaphoreType.DMA,
        ]

    def _copy(self, core, b, z, kind):
        p, n = self.p, self.p.depth
        ref = pair_of(self.buf, self.by_head, core, b, z)
        if kind == "right":
            return remote(ref, ref, self.send.at[z], self.recv.at[z], p.right)
        if kind == "left":
            return remote(ref, ref, self.send.at[n + z], self.recv.at[z], p.left)
        return remote(ref, ref, self.send.at[2 * n + z], self.recv.at[n + z], p.b_nbr)

    def _sib(self, core, b, z):
        n = self.p.depth
        ref = pair_of(self.buf, self.by_head, core, b, z)
        return remote(ref, ref, self.send.at[3 * n + b * n + z], self.recv.at[2 * n + b * n + z], self.p.sib)

    def start(self):
        self.keep.start()
        self.first.start()

    def _spread(self, core, z, right, left):
        p = self.p
        if right:
            pl.when(p.z < p.depth - 1)(lambda: self._copy(core, p.b, z, "right").start())
        if left:
            pl.when(p.z > 0)(lambda: self._copy(core, p.b, z, "left").start())
        self._copy(core, p.b, z, "b").start()
        self._sib(core, p.b, z).start()

    def along(self, k):
        p = self.p
        if isinstance(k, int) and k == 0:
            self.keep.wait()
            self.first.wait_recv()
            p.by_core(lambda core: self._spread(core, p.z, True, True))
            return

        def from_left(core):
            self._copy(core, p.b, p.z - k, "right").wait_recv()
            self._spread(core, p.z - k, True, False)

        def from_right(core):
            self._copy(core, p.b, p.z + k, "left").wait_recv()
            self._spread(core, p.z + k, False, True)

        pl.when(p.z - k >= 0)(lambda: p.by_core(from_left))
        pl.when(p.z + k < p.depth)(lambda: p.by_core(from_right))

    def across(self, k):
        p = self.p

        def one(z, core):
            self._copy(core, 1 - p.b, z, "b").wait_recv()
            self._sib(core, 1 - p.b, z).start()

        pl.when(p.z - k >= 0)(lambda: p.by_core(lambda core: one(p.z - k, core)))
        if not (isinstance(k, int) and k == 0):
            pl.when(p.z + k < p.depth)(lambda: p.by_core(lambda core: one(p.z + k, core)))

    def finish_at(self, z):
        def one(core):
            for b in (0, 1):
                self._sib(1 - core, b, z).wait_recv()

        self.p.by_core(one)

    def finish(self):
        each_of(self.p.depth, self.finish_at)

    def drain(self):
        p, n = self.p, self.p.depth
        self.first.wait_send()

        def each(z, carry):
            def one(core):
                pl.when(jnp.logical_and(p.z < n - 1, z <= p.z))(
                    lambda: self._copy(core, p.b, z, "right").wait_send()
                )
                pl.when(jnp.logical_and(p.z > 0, z >= p.z))(
                    lambda: self._copy(core, p.b, z, "left").wait_send()
                )
                self._copy(core, p.b, z, "b").wait_send()
                for b in (0, 1):
                    self._sib(core, b, z).wait_send()

            p.by_core(one)
            return carry

        lax.fori_loop(0, n, each, 0)


class Exchange:
    def __init__(self, p, src, dst, send, recv, own):
        m = p.m
        c, other = m % 2, 1 - m % 2
        self.local = [
            pltpu.make_async_copy(src.at[m], dst.at[m], own.at[0]),
            pltpu.make_async_copy(src.at[4 + c], dst.at[4 + c], own.at[1]),
            pltpu.make_async_copy(src.at[pl.ds(6, 2)], dst.at[pl.ds(6, 2)], own.at[2]),
        ]
        self.out = [
            remote(src.at[dev[1]], dst.at[m], send.at[j], recv.at[j], dev)
            for j, dev in enumerate(p.mp_peer)
        ] + [remote(src.at[4 + other], dst.at[4 + c], send.at[3], recv.at[3], p.sib)]

    @staticmethod
    def sems():
        return [
            pltpu.SemaphoreType.DMA((4,)),
            pltpu.SemaphoreType.DMA((4,)),
            pltpu.SemaphoreType.DMA((3,)),
        ]

    def start(self):
        for copy in self.out + self.local:
            copy.start()

    def finish(self):
        for copy in self.local:
            copy.wait()
        for copy in self.out:
            copy.wait_recv()

    def drain(self):
        for copy in self.out:
            copy.wait_send()


def add_rows(dst, src, rows):
    step = 32 if rows % 32 == 0 else 16

    def one(i, carry):
        at = pl.ds(pl.multiple_of(i * step, step), step)
        total = dst[at, :].astype(jnp.float32) + src[at, :].astype(jnp.float32)
        dst[at, :] = total.astype(dst.dtype)
        return carry

    lax.fori_loop(0, rows // step, one, 0)


class Scatter:
    def __init__(self, p, by_head, part, total, half, quarter, arrive, last, send, recv, mine=None, mine_sem=None, region=None):
        self.p, self.by_head, self.part, self.total = p, by_head, part, total
        self.mine, self.mine_sem, self.region = mine, mine_sem, region
        self.half, self.quarter, self.arrive, self.last = half, quarter, arrive, last
        self.send, self.recv = send, recv
        self.rows = part.shape[-2]

    @staticmethod
    def scratch(n, rows, cols, dtype=jnp.bfloat16):
        return [
            pltpu.VMEM((n, 2, 2, rows, cols), dtype),
            pltpu.VMEM((n, 2, rows, cols), dtype),
            pltpu.VMEM((n + 1, 2, rows, cols), dtype),
            pltpu.VMEM((rows, cols), dtype),
            pltpu.SemaphoreType.DMA((3 * n + 1,)),
            pltpu.SemaphoreType.DMA((3 * n + 2,)),
        ]

    def order(self, k):
        return self.p.order(k)

    def _region(self, core, z):
        if self.region is not None:
            return self.region(core, z)
        return self.part.at[:, core, z] if self.by_head else self.part.at[z, :, :, core]

    def _half_pair(self, core, b, z):
        over_first = (core == 0) != self.by_head
        return self.half.at[z, :, b] if over_first else self.half.at[z, b]

    def _sib(self, core, z):
        return remote(
            self._region(1 - core, z), self.half.at[z], self.send.at[z], self.recv.at[z], self.p.sib
        )

    def _b(self, core, z):
        n, p = self.p.depth, self.p
        return remote(
            self._half_pair(core, 1 - p.b, z), self.quarter.at[z], self.send.at[n + z], self.recv.at[n + z], p.b_nbr
        )

    def _right(self, z):
        n, p = self.p.depth, self.p
        return remote(
            self.quarter.at[z], self.arrive.at[z], self.send.at[2 * n + z], self.recv.at[2 * n + z], p.right
        )

    def _left(self, z, goal):
        n, p = self.p.depth, self.p
        return remote(
            self.quarter.at[z], self.arrive.at[goal], self.send.at[2 * n + z], self.recv.at[2 * n + goal], p.left
        )

    def _a(self):
        n, p = self.p.depth, self.p
        return remote(
            self.quarter.at[p.z, 1 - p.a], self.last, self.send.at[3 * n], self.recv.at[3 * n + 1], p.a_nbr
        )

    def _keep(self, core, z):
        return pltpu.make_async_copy(self._region(core, z), self.mine.at[z], self.mine_sem.at[z])

    def start(self, k):
        z = self.order(k)

        def one(core):
            self._sib(core, z).start()
            if self.mine is not None:
                self._keep(core, z).start()

        self.p.by_core(one)

    def to_half(self, k):
        z = self.order(k)

        def one(core):
            self._sib(core, z).wait_recv()
            region = self._region(core, z)
            if self.mine is not None:
                self._keep(core, z).wait()
                region = self.mine.at[z]
            for i in (0, 1):
                for j in (0, 1):
                    add_rows(self.half.at[z, i, j], region.at[i, j], self.rows)
            self._b(core, z).start()

        self.p.by_core(one)

    def to_quarter(self, k):
        z = self.order(k)

        def one(core):
            self._b(core, z).wait_recv()
            for i in (0, 1):
                add_rows(self.quarter.at[z, i], self._half_pair(core, self.p.b, z).at[i], self.rows)

        self.p.by_core(one)

    def _take(self, z, slot):
        for i in (0, 1):
            add_rows(self.quarter.at[z, i], self.arrive.at[slot, i], self.rows)

    def _send_left(self, z):
        p, n = self.p, self.p.depth
        pl.when(z == p.z - 1)(lambda: self._left(z, n).start())
        pl.when(z < p.z - 1)(lambda: self._left(z, z).start())

    def origin(self, k):
        p, n = self.p, self.p.depth
        z = self.order(k)
        pl.when(jnp.logical_and(p.z == 0, z > p.z))(lambda: self._right(z).start())
        pl.when(jnp.logical_and(p.z == n - 1, z < p.z))(lambda: self._send_left(z))

    def forward(self, k):
        p, n = self.p, self.p.depth
        z = self.order(k)

        def rightward():
            self._right(z).wait_recv()
            self._take(z, z)
            self._right(z).start()

        def leftward():
            self._left(z, z).wait_recv()
            self._take(z, z)
            self._send_left(z)

        pl.when(jnp.logical_and(p.z > 0, z > p.z))(rightward)
        pl.when(jnp.logical_and(p.z < n - 1, z < p.z))(leftward)

    def collect(self):
        p, n = self.p, self.p.depth

        def from_left():
            self._right(p.z).wait_recv()
            self._take(p.z, p.z)

        def from_right():
            self._left(p.z, n).wait_recv()
            self._take(p.z, n)

        pl.when(p.z > 0)(from_left)
        pl.when(p.z < n - 1)(from_right)
        self._a().start()

    def finish(self):
        p = self.p
        self._a().wait_recv()
        self.total[...] = self.quarter[p.z, p.a].astype(jnp.float32) + self.last[...].astype(jnp.float32)

    def drain(self):
        p, n = self.p, self.p.depth
        self._a().wait_send()

        def each(z, carry):
            def one(core):
                self._sib(core, z).wait_send()
                self._b(core, z).wait_send()

            p.by_core(one)
            pl.when(z != p.z)(lambda: self._right(z).wait_send())
            return carry

        lax.fori_loop(0, n, each, 0)

    def steps(self):
        n = self.p.depth
        todo = [lambda: [self.start(k) for k in range(n)]]
        todo += [functools.partial(self.to_half, k) for k in range(n)]
        for k in range(n):
            todo.append(functools.partial(lambda k: (self.to_quarter(k), self.origin(k), self.forward(k)), k))
        return todo


class Sum:
    def __init__(self, p, bits, value, slots, send, recv):
        self.p, self.bits, self.value, self.slots = p, bits, value, slots
        self.send, self.recv = send, recv

    @staticmethod
    def scratch(bits, rows):
        return [
            pltpu.VMEM((2 * (bits + 2), rows, 128), jnp.float32),
            pltpu.SemaphoreType.DMA((bits + 2,)),
            pltpu.SemaphoreType.DMA((bits + 2,)),
        ]

    def _copy(self, s):
        p = self.p
        dev = (p.sib, p.yn, *[p.flip(bit) for bit in range(self.bits)])[s]
        return remote(self.slots.at[2 * s], self.slots.at[2 * s + 1], self.send.at[s], self.recv.at[s], dev)

    def steps(self):
        def begin():
            self.slots[0] = self.value[...]
            self._copy(0).start()

        def one(s):
            self._copy(s).wait_recv()
            total = self.slots[2 * s] + self.slots[2 * s + 1]
            if s == self.bits + 1:
                self.value[...] = total
            else:
                self.slots[2 * s + 2] = total
                self._copy(s + 1).start()

        return [begin] + [functools.partial(one, s) for s in range(self.bits + 2)]

    def drain(self):
        for s in range(self.bits + 2):
            self._copy(s).wait_send()


def in_waves(lists, lag):
    for t in range(max(len(todo) + lag * r for r, todo in enumerate(lists))):
        for r, todo in enumerate(lists):
            if 0 <= t - lag * r < len(todo):
                todo[t - lag * r]()


def gather_kernel(p_depth, tok, cot, wq, wo, wi, wu, tok_s, cot_s, gq, go, gi, gu, *sems):
    p = Place(p_depth)
    n = p_depth
    arrays = []
    for i, (by_head, shard, buf) in enumerate(
        ((True, wq, gq), (False, wo, go), (False, wi, gi), (False, wu, gu))
    ):
        arrays.append(Gather(p, by_head, shard, buf, *sems[3 * i : 3 * i + 3]))
    rows = [Exchange(p, tok, tok_s, *sems[12:15]), Exchange(p, cot, cot_s, *sems[15:18])]
    p.barrier(0)
    for g in arrays:
        g.start()
    rows[0].start()
    if n <= 8:
        for k in range(n):
            for g in arrays:
                g.along(k)
            if k > 0:
                for g in arrays:
                    g.across(k - 1)
            if k == 1:
                rows[1].start()
        for g in arrays:
            g.across(n - 1)
    else:
        for g in arrays:
            g.along(0)
            lax.fori_loop(1, n, lambda k, carry: (g.along(k), carry)[1], 0)
        rows[1].start()
        for g in arrays:
            g.across(0)
            lax.fori_loop(1, n, lambda k, carry: (g.across(k), carry)[1], 0)
    for g in arrays + rows:
        g.finish()
    for g in arrays + rows:
        g.drain()


def gather_all(depth, tok, cot, shards):
    hbm = pl.BlockSpec(memory_space=pl.ANY)
    outs = [jax.ShapeDtypeStruct(tok.shape, tok.dtype)] * 2
    for i, s in enumerate(shards):
        lead = (2, 2, depth, 2) if i == 0 else (depth, 2, 2, 2)
        outs.append(jax.ShapeDtypeStruct(lead + s.shape, s.dtype))
    sems = Gather.sems(depth) * 4 + Exchange.sems() * 2
    return pl.pallas_call(
        functools.partial(gather_kernel, depth),
        out_shape=outs,
        in_specs=[hbm] * 6,
        out_specs=[hbm] * 6,
        scratch_shapes=sems,
        compiler_params=pltpu.CompilerParams(collective_id=0, has_side_effects=True),
        name="gather",
    )(tok, cot, *shards)


def scatter_kernel(depth, bits, pq, po, pi, pu, small, out_s, gtok_s, oq, oo, oi, ou, small_o, out, gtok, *scr):
    p = Place(depth)
    arrays = []
    for i, (by_head, part, total) in enumerate(
        ((False, pu, ou), (False, pi, oi), (False, po, oo), (True, pq, oq))
    ):
        arrays.append(Scatter(p, by_head, part, total, *scr[6 * i : 6 * i + 6]))
    rows = [Exchange(p, out_s, out, *scr[24:27]), Exchange(p, gtok_s, gtok, *scr[27:30])]
    small_o[...] = small[...]
    sums = Sum(p, bits, small_o, *scr[30:33])
    p.barrier(bits)
    rows[0].start()
    in_waves([g.steps() for g in arrays], min(depth, 4))
    rows[1].start()
    close(arrays, sums)
    for r in rows:
        r.finish()
    for g in arrays + rows + [sums]:
        g.drain()


def close(arrays, sums):
    closing = [g.collect for g in arrays] + [g.finish for g in arrays]
    for step in itertools.chain(*itertools.zip_longest(sums.steps(), closing)):
        if step is not None:
            step()


def scatter_all(depth, bits, parts, small, out_s, gtok_s):
    hbm = pl.BlockSpec(memory_space=pl.ANY)
    vmem = pl.BlockSpec(memory_space=pltpu.VMEM)
    outs = [jax.ShapeDtypeStruct(s.shape[4:], jnp.float32) for s in parts]
    outs += [jax.ShapeDtypeStruct(small.shape, jnp.float32)]
    outs += [jax.ShapeDtypeStruct(out_s.shape, out_s.dtype)] * 2
    scr = []
    for s in (parts[3], parts[2], parts[1], parts[0]):
        scr += Scatter.scratch(depth, *s.shape[4:])
    scr += Exchange.sems() * 2 + Sum.scratch(bits, small.shape[0])
    return pl.pallas_call(
        functools.partial(scatter_kernel, depth, bits),
        out_shape=outs,
        in_specs=[vmem] * 5 + [hbm] * 2,
        out_specs=[vmem] * 5 + [hbm] * 2,
        scratch_shapes=scr,
        compiler_params=pltpu.CompilerParams(
            collective_id=1, has_side_effects=True, vmem_limit_bytes=60 * 2**20
        ),
        name="scatter",
    )(*parts, small, out_s, gtok_s)

SPANS = ((0, LEN_LONG), (LEN_LONG, LEN_MID), (LEN_LONG + LEN_MID, LEN_SHORT), (LEN_LONG + LEN_MID + LEN_SHORT, LEN_SHORT))
TILE = 128
QKV_PAD = 640
CTX_PAD = 256
ADAPT_PAD = 128
MASK_LOW = -1e9
NN = (((1,), (0,)), ((), ()))
NT = (((1,), (1,)), ((), ()))
TN = (((0,), (0,)), ((), ()))


def dot(a, b, dims=NN):
    return lax.dot_general(a, b, dims, preferred_element_type=jnp.float32)


def table_onehot():
    buckets = rel_buckets(257)
    offset = np.clip(256 - np.arange(512), -256, 256) + 256
    index = np.concatenate([buckets[offset], np.full(128, NB // 2 - 1), np.full(128, NB - 1)])
    return (index[:, None] == np.arange(NB)[None, :]).astype(np.float32)


def bias_tiles(row):
    spread = pltpu.roll(jnp.broadcast_to(row, (TILE, 512)), 0, 1, stride=1, stride_axis=0)
    far = [jnp.broadcast_to(row[:, at : at + 1], (TILE, TILE)) for at in (511, 0)]
    near = [spread[:, 256 - 128 * delta : 384 - 128 * delta] for delta in (-1, 0, 1)]
    return [far[0], *near, far[1]]


def diagonal_sums(tiles):
    grid = jnp.concatenate([jnp.zeros((TILE, TILE), jnp.float32), tiles[2], tiles[1], tiles[0]], axis=1)
    rows = TILE
    while rows > 8:
        rows //= 2
        grid = grid[:rows] + pltpu.roll(grid[rows:], 512 - rows, 1)
    total = grid[0:1]
    for r in range(1, 8):
        total = total + pltpu.roll(grid[r : r + 1], 512 - r, 1)
    return total


def swap_halves(tile):
    return jnp.concatenate([tile[:, DH:], tile[:, :DH]], axis=1)


def lanes_below(shape, at=DH):
    return lax.broadcasted_iota(jnp.int32, shape, len(shape) - 1) < at


def key_side(qk, mask):
    swapped = swap_halves(qk)
    return jnp.where(lanes_below(qk.shape), swapped, mask), swapped


def query_side(qk):
    lane = lax.broadcasted_iota(jnp.int32, qk.shape, 1)
    return jnp.where(lane < DH, qk, jnp.where(lane == DH, 1.0, 0.0).astype(qk.dtype))


def probabilities(scores, tiles, length, q0=0):
    width = scores.shape[1]
    blocks = []
    for kb in range(length // TILE):
        deltas = [max(-2, min(2, kb - (q0 + qi))) + 2 for qi in range(width // TILE)]
        bias = tiles[deltas[0]] if len(deltas) == 1 else jnp.concatenate([tiles[d] for d in deltas], axis=1)
        blocks.append(scores[kb * TILE : (kb + 1) * TILE] + bias)
    top = blocks[0]
    for block in blocks[1:]:
        top = jnp.maximum(top, block)
    top = jnp.max(top, axis=0, keepdims=True)
    blocks = [jnp.exp(block - top) for block in blocks]
    total = blocks[0]
    for block in blocks[1:]:
        total = total + block
    inverse = 1.0 / jnp.sum(total, axis=0, keepdims=True)
    return [block * inverse for block in blocks]


def join(blocks, axis=0):
    return blocks[0] if len(blocks) == 1 else jnp.concatenate(blocks, axis=axis)


def value_lanes(group):
    stride = group * CTX_PAD // (3 * DH)
    lane = np.arange(CTX_PAD)
    column = lane // stride * group + lane % stride
    return np.where(lane % stride < group, column // DH, -1), column


def head_runs(group):
    heads, _ = value_lanes(group)
    runs = []
    for lane in range(CTX_PAD):
        head = int(heads[lane])
        head = runs[-1][2] if head < 0 else head
        if runs and runs[-1][2] == head:
            runs[-1][1] = lane + 1
        else:
            runs.append([lane, lane + 1, head])
    return runs


def head_lanes(shape, group, head):
    lane = lax.broadcasted_iota(jnp.int32, shape, len(shape) - 1)
    inside = None
    for lo, hi, h in head_runs(group):
        if h == head:
            run = jnp.logical_and(lane >= lo, lane < hi)
            inside = run if inside is None else jnp.logical_or(inside, run)
    return inside


def no_tick(j):
    pass


def no_keep(number, place, h, probs):
    pass


FRONT_SPANS = (SPANS[:1], SPANS[1:])
FRONT_WIDTH = 256


def attend_group(packed, mask_ref, rows, context, group, tick=no_tick, keep=no_keep):
    tiles = [bias_tiles(rows[h : h + 1, :]) for h in range(3)]
    for number, spans in enumerate(FRONT_SPANS):
        units = []
        for offset, length in spans:
            width = min(length, FRONT_WIDTH)
            units += [(offset, length, q0, width) for q0 in range(0, length, width)]
        batches = [[unit] for unit in units] if number == 0 else [units]
        keys = {
            (offset, h): key_side(packed[pl.ds(offset, length), h * TILE : (h + 1) * TILE], mask_ref[pl.ds(offset, length), :])[0]
            for offset, length in spans
            for h in range(3)
        }
        values = {offset: packed[pl.ds(offset, length), 3 * TILE : QKV_PAD].T for offset, length in spans}
        for turn, batch in enumerate(batches):
            work = [(unit, h) for unit in batch for h in range(3)]
            scores = []
            for (offset, length, q0, width), h in work:
                queries = query_side(packed[pl.ds(offset + q0, width), h * TILE : (h + 1) * TILE])
                scores.append(dot(keys[offset, h], queries, NT))
            probs = []
            for ((offset, length, q0, width), h), score in zip(work, scores):
                blocks = probabilities(score, tiles[h], length, q0 // TILE)
                probs.append(join([block.astype(jnp.bfloat16) for block in blocks]))
            for (unit, h), prob in zip(work, probs):
                keep(number, unit, h, prob)
            outs = [dot(values[unit[0]], prob) for (unit, h), prob in zip(work, probs)]
            for i, (offset, length, q0, width) in enumerate(batch):
                own = outs[3 * i : 3 * i + 3]
                whole = jnp.concatenate([own[h][lo:hi] for lo, hi, h in head_runs(group)], axis=0)
                context[pl.ds(offset + q0, width), :] = whole.T.astype(jnp.bfloat16)
            tick((number, turn))


BACK_SPANS = (SPANS[:1], SPANS[1:])
SKEW = (5, 0)


def head_back(packed, recall, grad_context, grad_packed, group, near, far, value_sums, span_of, h):
    offset, length = span_of
    span, at = pl.ds(offset, length), pl.ds(h * TILE, TILE)
    qk = packed[span, at]
    low = lanes_below(qk.shape)
    swapped = swap_halves(qk)
    g_tile = grad_context[span, :]
    g_tile = jnp.where(head_lanes(g_tile.shape, group, h), g_tile, jnp.zeros_like(g_tile))
    scores = recall.scores(qk, span, h)
    g_probs = dot(packed[span, 3 * TILE : QKV_PAD], g_tile, NT)
    yield
    probs = recall.probs(scores, span_of, h)
    yield
    count = length // TILE
    g_blocks = [g_probs[kb * TILE : (kb + 1) * TILE] for kb in range(count)]
    total = probs[0] * g_blocks[0]
    for kb in range(1, count):
        total = total + probs[kb] * g_blocks[kb]
    centre = jnp.sum(total, axis=0, keepdims=True)
    low_probs = join([block.astype(jnp.bfloat16) for block in probs])
    g_scores = [(a * (g - centre)).astype(jnp.bfloat16) for a, g in zip(probs, g_blocks)]
    for kb, block in enumerate(g_scores):
        wide = block.astype(jnp.float32)
        for qi in range(count):
            piece = wide[:, qi * TILE : (qi + 1) * TILE]
            delta = kb - qi
            if abs(delta) <= 1:
                held = near[h][delta + 1]
                near[h][delta + 1] = piece if held is None else held + piece
            else:
                side = 0 if delta < 0 else 1
                far[h][side] = far[h][side] + piece
    yield
    g_scores = join(g_scores)
    g_v = dot(low_probs, g_tile)
    value_sums[offset] = value_sums[offset] + g_v if offset in value_sums else g_v
    grad_keys = dot(g_scores, jnp.where(low, jnp.zeros_like(qk), swapped))
    grad_queries = dot(jnp.where(low, swapped, jnp.zeros_like(qk)).T, g_scores).T
    yield
    grad_packed[span, at] = (grad_queries + grad_keys).astype(jnp.bfloat16)


class Again:
    def __init__(self, mask, rows):
        self.mask = mask
        self.tiles = [bias_tiles(rows[h : h + 1, :]) for h in range(3)]

    def scores(self, qk, span, h):
        return dot(key_side(qk, self.mask[span, :])[0], query_side(qk), NT)

    def probs(self, scores, span_of, h):
        return probabilities(scores, self.tiles[h], span_of[1])


class Kept:
    def __init__(self, kept):
        self.kept = kept

    def scores(self, qk, span, h):
        return None

    def probs(self, scores, span_of, h):
        offset, length = span_of
        pieces = [self.kept[r : r + n, c : c + w] for r, n, c, w in kept_at(offset, length, h)]
        whole = join(pieces, axis=1).astype(jnp.float32)
        return [whole[kb * TILE : (kb + 1) * TILE] for kb in range(length // TILE)]


KEPT_LONG, KEPT_REST = 1024, 384


def kept_at(offset, length, h):
    if length == LEN_LONG:
        if h < 2:
            return [(LEN_LONG * h, LEN_LONG, 0, LEN_LONG)]
        return [(LEN_LONG * k, LEN_LONG, LEN_LONG, LEN_LONG // 2) for k in range(2)]
    if length == LEN_MID:
        return [(KEPT_LONG, LEN_MID, LEN_MID * h, LEN_MID)]
    second = (offset - LEN_LONG - LEN_MID) // LEN_SHORT
    return [(KEPT_LONG + LEN_MID, LEN_SHORT, LEN_SHORT * (3 * second + h), LEN_SHORT)]


def attend_group_back(packed, recall, grad_context, grad_packed, sums, group, tick=no_tick):
    near = [[None] * 3 for _ in range(3)]
    far = [[jnp.zeros((TILE, TILE), jnp.float32)] * 2 for _ in range(3)]
    value_sums = {}

    def heads_of(spans):
        return [
            head_back(packed, recall, grad_context, grad_packed, group, near, far, value_sums, s, h)
            for s in spans
            for h in range(3)
        ]

    def values_of(spans):
        for offset, length in spans:
            grad_packed[pl.ds(offset, length), 3 * TILE : QKV_PAD] = value_sums.pop(offset).astype(jnp.bfloat16)

    for number, spans in enumerate(BACK_SPANS):
        heads = heads_of(spans)
        skew = SKEW[number]
        for t in range(5 + skew * (len(heads) - 1)):
            for i, head in enumerate(heads):
                if 0 <= t - skew * i < 5:
                    next(head, None)
                    if t - skew * i == 4:
                        tick((number, i))
        values_of(spans)
    for h in range(3):
        sums[h : h + 1, :512] = diagonal_sums(near[h])
        for side in range(2):
            sums[h : h + 1, 512 + side * TILE : 640 + side * TILE] = jnp.sum(far[h][side], axis=0, keepdims=True)


def attention_kernel(group, x_ref, gain, w_ref, mask, rows, normed_out, packed, context):
    @pl.when(pl.program_id(0) == 0)
    def _():
        x = x_ref[...].astype(jnp.float32)
        scale = lax.rsqrt(jnp.mean(x * x, axis=-1, keepdims=True) + NORM_EPS)
        normed_out[...] = (x * scale * gain[...]).astype(jnp.bfloat16)

    packed[0] = dot(normed_out[...], w_ref[0]).astype(jnp.bfloat16)
    attend_group(packed.at[0], mask, rows[0], context.at[0], group)


def attention(x, gain, w, mask, rows, group):
    n = x.shape[0]
    bf = jnp.bfloat16
    return pl.pallas_call(
        functools.partial(attention_kernel, group),
        grid=(4,),
        out_shape=[
            jax.ShapeDtypeStruct((n, D), bf),
            jax.ShapeDtypeStruct((4, n, QKV_PAD), bf),
            jax.ShapeDtypeStruct((4, n, CTX_PAD), bf),
        ],
        in_specs=[
            pl.BlockSpec((n, D), lambda i: (0, 0)),
            pl.BlockSpec((1, D), lambda i: (0, 0)),
            pl.BlockSpec((1, D, QKV_PAD), lambda i: (i, 0, 0)),
            pl.BlockSpec((n, TILE), lambda i: (0, 0)),
            pl.BlockSpec((1, 3, 512), lambda i: (i, 0, 0)),
        ],
        out_specs=[
            pl.BlockSpec((n, D), lambda i: (0, 0)),
            pl.BlockSpec((1, n, QKV_PAD), lambda i: (i, 0, 0)),
            pl.BlockSpec((1, n, CTX_PAD), lambda i: (i, 0, 0)),
        ],
        compiler_params=pltpu.CompilerParams(vmem_limit_bytes=56 * 2**20),
        name="attention",
    )(x, gain, w, mask, rows)


def attention_back_kernel(group, packed, grad_context, mask, rows, grad_packed, sums):
    attend_group_back(packed.at[0], Again(mask, rows[0]), grad_context.at[0], grad_packed.at[0], sums.at[0], group)


def attention_back(packed, grad_context, mask, rows, group):
    n = packed.shape[1]
    return pl.pallas_call(
        functools.partial(attention_back_kernel, group),
        grid=(4,),
        out_shape=[
            jax.ShapeDtypeStruct((4, n, QKV_PAD), jnp.bfloat16),
            jax.ShapeDtypeStruct((4, 3, 768), jnp.float32),
        ],
        in_specs=[
            pl.BlockSpec((1, n, QKV_PAD), lambda i: (i, 0, 0)),
            pl.BlockSpec((1, n, CTX_PAD), lambda i: (i, 0, 0)),
            pl.BlockSpec((n, TILE), lambda i: (0, 0)),
            pl.BlockSpec((1, 3, 512), lambda i: (i, 0, 0)),
        ],
        out_specs=[
            pl.BlockSpec((1, n, QKV_PAD), lambda i: (i, 0, 0)),
            pl.BlockSpec((1, 3, 768), lambda i: (i, 0, 0)),
        ],
        compiler_params=pltpu.CompilerParams(vmem_limit_bytes=56 * 2**20),
        name="attention_back",
    )(packed, grad_context, mask, rows)


def head_columns(w, group):
    n = w.shape[0]
    qk = w[:, :, : 2 * DH].reshape(n, 6 * DH)
    v = w[:, :, 2 * DH :].reshape(n, 3 * DH // group, group)
    v = jnp.pad(v, ((0, 0), (0, 0), (0, group // 3))).reshape(n, CTX_PAD)
    return jnp.concatenate([qk, v], axis=1)


def key_mask(live):
    lane = jnp.arange(TILE)[None, :]
    return jnp.where((lane == DH) & ~live[:, None], MASK_LOW, 0.0).astype(jnp.bfloat16)


def precise(a, b, dims=NN):
    return lax.dot_general(a, b, dims, precision=FULL_PRECISION, preferred_element_type=jnp.float32)


def offset_onehot():
    buckets = rel_buckets(257)
    offset = np.clip(256 - np.arange(512), -256, 256) + 256
    return (np.arange(NB)[:, None] == buckets[offset][None, :]).astype(np.float32)


def column_choice(group):
    choice = np.zeros((9 * DH, QKV_PAD), np.float32)
    for h in range(3):
        for k in range(2 * DH):
            choice[3 * DH * h + k, TILE * h + k] = 1
    heads, column = value_lanes(group)
    for lane in range(CTX_PAD):
        if heads[lane] >= 0:
            choice[3 * DH * heads[lane] + 2 * DH + column[lane] % DH, 3 * TILE + lane] = 1
    return choice


def own_length(lengths, member, number):
    at = (member, 4 + member // 2 + 2 * (member % 2), 8 + member, 12 + member)[number]
    return lengths[at]


def fill_mask(mask, lengths, member):
    for number, (offset, length) in enumerate(SPANS):
        row = lax.broadcasted_iota(jnp.int32, (length, TILE), 0)
        lane = lax.broadcasted_iota(jnp.int32, (length, TILE), 1)
        dead = jnp.logical_and(row >= own_length(lengths, member, number), lane == DH)
        mask[offset : offset + length, :] = jnp.where(dead, MASK_LOW, 0.0).astype(jnp.bfloat16)


def fill_rows(rows, pos_table, onehot):
    table = precise(pos_table[...], onehot[...])
    for m in range(4):
        rows[m] = table[3 * m : 3 * m + 3, :]


KA = ADAPT // KRON


def adapter_constants():
    i, b = np.arange(16) // 4, np.arange(16) % 4
    same = (np.arange(4)[:, None] == i[None, :]).astype(np.float32)
    pick = np.zeros((4, 4, 16), np.float32)
    pick[i, b, np.arange(16)] = 1
    fold = np.zeros((ADAPT_PAD, KA), np.float32)
    fold[np.arange(ADAPT), np.arange(ADAPT) % KA] = 1
    agree = np.zeros((ADAPT_PAD, 16), np.float32)
    agree[:ADAPT] = np.arange(ADAPT)[:, None] // KA == b[None, :]
    return same, pick, fold, agree


class Factor:
    def __init__(self, rules, tall, short, consts):
        self.same, _, self.fold, self.agree = consts
        spread = precise(tall, self.same, TN)
        self.tall = jnp.concatenate([spread] * KRON, axis=0)
        rows = spread.shape[0]
        self.rules = jnp.concatenate(
            [jnp.broadcast_to(rules[a : a + 1, :], (rows, 16)) for a in range(KRON)], axis=0
        )
        self.short = precise(self.fold, precise(short, self.same, TN)) * self.agree

    def whole(self):
        return precise(self.rules * self.tall, self.short, NT)

    def back(self, grad):
        wide = precise(grad, self.short)
        rows = wide.shape[0] // KRON
        tall = wide * self.rules
        tall = sum(tall[a * rows : (a + 1) * rows] for a in range(KRON))
        rules = wide * self.tall
        rules = [jnp.sum(rules[a * rows : (a + 1) * rows], axis=0, keepdims=True) for a in range(KRON)]
        short = precise(self.rules * self.tall, grad, TN) * self.agree.T
        short = precise(precise(self.same, short), self.fold)
        return jnp.concatenate(rules, axis=0), precise(self.same, tall, NT), short


def rule_tables(rules, pick):
    return [sum(precise(rules[i], pick[i], dims) for i in range(KRON)) for dims in (NN, TN)]


ROW_GAIN, ROW_TABLE, ROW_OTHER = 0, 8, 24
ROW_FFN, ROW_DL, ROW_UR, ROW_DR, ROW_UL, ROW_RULES, ROW_END = 0, 8, 16, 24, 28, 32, 48


def put_row(ref, at, row):
    for k in range(row.shape[1] // 128):
        ref[at + k : at + k + 1, :] = row[:, 128 * k : 128 * (k + 1)]


FCH = 768
RCH = 256


def gelu_both(v):
    phi = 0.5 + 0.5 * lax.erf(v * np.float32(np.sqrt(0.5)))
    return v * phi, phi + v * (jnp.exp(-0.5 * v * v) * np.float32(1.0 / np.sqrt(2.0 * np.pi)))


def rows_of(i, size=RCH):
    return pl.ds(pl.multiple_of(i * size, size), size)


def each_of(count, body):
    lax.fori_loop(0, count, lambda i, carry: (body(i), carry)[1], 0)


class Layer:
    def __init__(self, **refs):
        self.__dict__.update(refs)
        self.n = self.n2.shape[0]

    def midway(self, i):
        r = rows_of(i)
        total = self.x_rows(i)
        for m in range(4):
            total = total + dot(self.ctx[m, r, :], self.wo(m))
        self.mid[r, :] = total
        scale = lax.rsqrt(jnp.mean(total * total, axis=-1, keepdims=True) + NORM_EPS)
        self.n2[r, :] = (total * scale * self.gain[...]).astype(jnp.bfloat16)

    def forward(self, j):
        f = rows_of(j, self.chunk)
        for half in range(2):
            r = pl.ds(half * (self.n // 2), self.n // 2)
            value, slope = gelu_both(dot(self.n2[r, :], self.wi(j), NT))
            value = value.astype(jnp.bfloat16)
            self.act[r, f] = value
            self.dg[r, f] = slope.astype(jnp.bfloat16)
            self.acc[r, :] += dot(value, self.wu(j))

    def factors(self):
        consts = [c[...] for c in self.consts]
        by_a, by_b = rule_tables(self.rules, consts[1])
        d_left, d_right, u_left, u_right = self.sides
        return (
            Factor(by_a, d_left[...], d_right[...], consts),
            Factor(by_b, u_right[...], u_left[...], consts),
        )

    def prepare(self, member):
        down, up = self.factors()
        self.down[...] = down.whole().astype(jnp.bfloat16)
        self.up[...] = up.whole().astype(jnp.bfloat16)
        for number, (offset, length) in enumerate(SPANS):
            row = lax.broadcasted_iota(jnp.int32, (length, 1), 0)
            alive = row < own_length(self.lengths, member, number)
            self.live[offset : offset + length, :] = jnp.where(alive, 1.0, 0.0)

    def adapter(self, i):
        bf = jnp.bfloat16
        r = rows_of(i)
        ffn = self.acc[r, :]
        low = ffn.astype(bf)
        value, slope = gelu_both(dot(low, self.down[...]))
        value = value.astype(bf)
        self.put_res(i, (self.mid[r, :] + ffn + dot(value, self.up[...], NT)).astype(bf))
        g_out = self.cot_rows(i) * self.live[r, :]
        g_low = g_out.astype(bf)
        self.gout[r, :] = g_low
        g_sq = (dot(g_low, self.up[...]) * slope).astype(bf)
        self.g_up[...] += dot(g_low, value, TN)
        self.g_down[...] += dot(low, g_sq, TN)
        self.gffn[r, :] = (g_out + dot(g_sq, self.down[...], NT)).astype(bf)

    def backward(self, j):
        dg = self.slope(j)
        for half in range(2):
            r = pl.ds(half * (self.n // 2), self.n // 2)
            g = (dot(self.gffn[r, :], self.wu(j), NT) * dg[r, :].astype(jnp.float32)).astype(jnp.bfloat16)
            dg[r, :] = g
            self.acc[r, :] += dot(g, self.wi(j))

    def last(self, i):
        r = rows_of(i)
        total = self.mid[r, :]
        g_n2 = self.acc[r, :]
        scale = lax.rsqrt(jnp.mean(total * total, axis=-1, keepdims=True) + NORM_EPS)
        self.g_gain[...] += jnp.sum(total * scale * g_n2, axis=0, keepdims=True)
        scaled = self.gain[...] * g_n2
        centre = jnp.mean(total * scaled, axis=-1, keepdims=True)
        g_mid = self.gout[r, :].astype(jnp.float32) + scale * scaled - total * (scale * scale * scale * centre)
        self.mid[r, :] = g_mid
        self.glow[r, :] = g_mid.astype(jnp.bfloat16)

    def projection(self, m):
        grad = dot(self.ctx[m], self.glow[...], TN).astype(jnp.bfloat16)
        self.ctx[m] = dot(self.glow[...], self.wo(m), NT).astype(jnp.bfloat16)
        return grad

    def adapter_all(self):
        self.g_down[...] = jnp.zeros_like(self.g_down)
        self.g_up[...] = jnp.zeros_like(self.g_up)
        each_of(self.n // RCH, self.adapter)

    def adapter_grads(self):
        other, pick = self.other, self.consts[1]
        down, up = self.factors()
        g_a, g_dl, g_dr = down.back(self.g_down[...])
        g_b, g_ur, g_ul = up.back(self.g_up[...])
        other[...] = jnp.zeros_like(other)
        for at, tall in ((ROW_DL, g_dl), (ROW_UR, g_ur)):
            other[at : at + 4, :] = tall[:, :128]
            other[at + 4 : at + 8, : tall.shape[1] - 128] = tall[:, 128:]
        for at, short in ((ROW_DR, g_dr), (ROW_UL, g_ul)):
            other[at : at + 4, :KA] = short
        for i in range(KRON):
            at = ROW_RULES + 4 * i
            other[at : at + 4, :KRON] = precise(g_a, pick[i], NT) + precise(pick[i], g_b, NT)


def middle_kernel(
    x_hbm, ctx_hbm, wo_hbm, wi_hbm, wu_hbm, cot_hbm, gain, lengths, rules, d_left, d_right, u_left, u_right,
    same, pick, fold, agree,
    res_hbm, gmid_hbm, gctx_hbm, go_hbm, gi_hbm, gu_hbm, other,
    down, up, g_down, g_up, g_gain, live, x, ctx, wo, wi, wu, cot, mid, n2, act, dg, acc, gffn, glow, sem, sems, out_sems,
):
    gain = gain[...].reshape(1, D)
    loads = [
        pltpu.make_async_copy(src, dst, sems.at[i])
        for i, (src, dst) in enumerate(
            ((x_hbm, x), (ctx_hbm, ctx), (wo_hbm, wo), (wi_hbm, wi), (wu_hbm, wu), (cot_hbm, cot))
        )
    ]
    for load in loads:
        load.start()
    def put_res(i, value):
        x[rows_of(i), :] = value

    layer = Layer(
        x_rows=lambda i: x[rows_of(i), :].astype(jnp.float32), cot_rows=lambda i: cot[rows_of(i), :].astype(jnp.float32),
        wo=lambda m: wo[m], wi=lambda j: wi[rows_of(j, FCH), :], wu=lambda j: wu[rows_of(j, FCH), :],
        chunk=FCH, ctx=ctx, gain=gain, lengths=lengths, rules=rules, sides=(d_left, d_right, u_left, u_right),
        consts=(same, pick, fold, agree), down=down, up=up, g_down=g_down, g_up=g_up, g_gain=g_gain, live=live, mid=mid,
        n2=n2, act=act, dg=dg, acc=acc, gffn=gffn, glow=glow, put_res=put_res, gout=cot, other=other,
        slope=lambda j: dg.at[:, rows_of(j, FCH)],
    )
    layer.prepare(lax.axis_index("mp"))
    for load in loads:
        load.wait()
    each_of(layer.n // RCH, layer.midway)
    acc[...] = jnp.zeros_like(acc)
    count = wi.shape[0] // FCH
    each_of(count, layer.forward)
    layer.adapter_all()
    acc[...] = jnp.zeros_like(acc)
    g_gain[...] = jnp.zeros_like(g_gain)

    def stores(j):
        f = rows_of(j, FCH)
        return [
            pltpu.make_async_copy(src.at[pl.ds(0, FCH), f], dst.at[f], sem.at[k, j])
            for k, (src, dst) in enumerate(((act, gu_hbm), (dg, gi_hbm)))
        ]

    def backward(j):
        f = rows_of(j, FCH)
        layer.backward(j)
        act[:FCH, f] = dot(act[:, f], gffn[...], TN).astype(jnp.bfloat16)
        dg[:FCH, f] = dot(dg[:, f], n2[...], TN).astype(jnp.bfloat16)
        for store in stores(j):
            store.start()

    each_of(count, backward)
    each_of(layer.n // RCH, layer.last)
    for m in range(4):
        gffn[CTX_PAD * m : CTX_PAD * (m + 1), :] = layer.projection(m)
    layer.adapter_grads()
    put_row(other, ROW_FFN, g_gain[...])
    copies = [
        pltpu.make_async_copy(src, dst, out_sems.at[k])
        for k, (src, dst) in enumerate(((x, res_hbm), (mid, gmid_hbm), (gffn, go_hbm), (ctx, gctx_hbm)))
    ]
    for copy in copies:
        copy.start()
    each_of(count, lambda j: [store.wait() for store in stores(j)])
    for copy in copies:
        copy.wait()


def middle(x, ctx, wo, wi, wu, cot, gain, lengths, factors):
    n, ff = x.shape[0], wi.shape[0]
    bf, f32 = jnp.bfloat16, jnp.float32
    hbm = pl.BlockSpec(memory_space=pl.ANY)
    vmem = pl.BlockSpec(memory_space=pltpu.VMEM)
    shape = jax.ShapeDtypeStruct
    return pl.pallas_call(
        middle_kernel,
        out_shape=[
            shape((n, D), bf),
            shape((n, D), f32),
            shape((4, n, CTX_PAD), bf),
            shape((4 * CTX_PAD, D), bf),
            shape((ff, D), bf),
            shape((ff, D), bf),
            shape((ROW_END, 128), f32),
        ],
        in_specs=[hbm] * 6 + [vmem] + [pl.BlockSpec(memory_space=pltpu.SMEM)] + [vmem] * 9,
        out_specs=[hbm] * 6 + [vmem],
        scratch_shapes=[
            pltpu.VMEM((D, ADAPT_PAD), bf),
            pltpu.VMEM((D, ADAPT_PAD), bf),
            pltpu.VMEM((D, ADAPT_PAD), f32),
            pltpu.VMEM((D, ADAPT_PAD), f32),
            pltpu.VMEM((1, D), f32),
            pltpu.VMEM((n, 1), f32),
            pltpu.VMEM((n, D), bf),
            pltpu.VMEM((4, n, CTX_PAD), bf),
            pltpu.VMEM((4, CTX_PAD, D), bf),
            pltpu.VMEM((ff, D), bf),
            pltpu.VMEM((ff, D), bf),
            pltpu.VMEM((n, D), bf),
            pltpu.VMEM((n, D), f32),
            pltpu.VMEM((n, D), bf),
            pltpu.VMEM((n, ff), bf),
            pltpu.VMEM((n, ff), bf),
            pltpu.VMEM((n, D), f32),
            pltpu.VMEM((n, D), bf),
            pltpu.VMEM((n, D), bf),
            pltpu.SemaphoreType.DMA((2, ff // FCH)),
            pltpu.SemaphoreType.DMA((6,)),
            pltpu.SemaphoreType.DMA((4,)),
        ],
        compiler_params=pltpu.CompilerParams(vmem_limit_bytes=63 * 2**20),
        name="middle",
    )(x, ctx, wo, wi, wu, cot, gain, lengths, *factors, *map(jnp.asarray, adapter_constants()))


FRONT = (
    "s:o s:q ex0 a:o0",
    "s:i a:q0 a:q1 a:q2",
    "c:q0 a:o1 c:q1 a:i0",
    "c:o0 a:q3 s:u n",
    "c:q2 a:o2 ex1 c:q3",
    "f:q a:u0 A A",
    "A c:o1 A a:i1",
    "a:o3 c:i0 A c:o2",
    "a:u1 A A A",
    "A A a:i2 c:o3",
    "A c:u0 A c:i1",
    "f:o O c:u1 a:u2",
    "c:i2 F0 a:i3 F1",
    "c:u2 a:u3 c:i3 F2",
    "c:u3 F3",
)


def front_order():
    plan, now = {"first": []}, "first"
    pieces = 0
    for step in " ".join(FRONT).split():
        if step == "A":
            now, pieces = ("A", pieces), pieces + 1
        elif step[0] in "OF":
            plan["before", step] = plan.pop("open", [])
            now = "open"
        else:
            plan.setdefault(now, []).append(step)
    return plan


def front_kernel(
    depth, group, tok, cot, w_qkv, w_o, w_in, w_out, choice, gain, gain_ffn, lengths, pos_table, onehot,
    rules, d_left, d_right, u_left, u_right, same, pick, fold, agree,
    tok_s, gq_hbm, normed_hbm, packed_hbm, out, mid_hbm, ctx_hbm, go_hbm, gi_hbm, gu_hbm, dg_hbm, pu_hbm, gffn_hbm, n2_hbm,
    gout_hbm, long_hbm, rest_hbm, other,
    wq, wo, wi, wu, mask, rows, x, y, gq, go, gi, gu, nrm, packed, ctx,
    down, up, g_down, g_up, live, mid, n2, act, dg, acc, gffn, res, sem, out_sems, local, *sems,
):
    p = Place(depth)
    bf = jnp.bfloat16
    p.greet(0)
    gain, gain_ffn = gain[...].reshape(1, D), gain_ffn[...].reshape(1, D)
    per_head = [dot(w_qkv[h].astype(bf), choice[3 * DH * h : 3 * DH * (h + 1), :]) for h in range(3)]
    wq[...] = sum(per_head).astype(bf)
    wo[...] = jnp.zeros_like(wo)
    wo[: w_o.shape[0], :] = w_o[...].astype(bf)
    wi[...] = w_in[...].astype(bf)
    wu[...] = w_out[...].astype(bf)
    arrays = {
        name: Gather(p, name == "q", shard, buf, *sems[3 * i : 3 * i + 3])
        for i, (name, shard, buf) in enumerate((("q", wq, gq), ("o", wo, go), ("i", wi, gi), ("u", wu, gu)))
    }
    first, second = Exchange(p, tok, x, *sems[12:15]), Exchange(p, cot, y, *sems[15:18])
    keep_x = pltpu.make_async_copy(x, tok_s, local.at[0])
    keep_n = pltpu.make_async_copy(nrm, normed_hbm, local.at[1])
    keep_q = pltpu.make_async_copy(gq, gq_hbm, local.at[2])
    quarter = RCH // SEG

    def float_rows(ref):
        return lambda i: ref[pl.ds(quarter * i, quarter)].reshape(RCH, D).astype(jnp.float32)

    def put_res(i, value):
        res[pl.ds(quarter * i, quarter)] = value.reshape(quarter, SEG, D)

    chunk_rows = 8 * wi.shape[0]
    layer = Layer(
        x_rows=float_rows(x), cot_rows=float_rows(y),
        wo=lambda m: go[m].reshape(CTX_PAD, D), wi=lambda j: gi[j].reshape(-1, D), wu=lambda j: gu[j].reshape(-1, D),
        chunk=chunk_rows, ctx=ctx, gain=gain_ffn, lengths=lengths, rules=rules, sides=(d_left, d_right, u_left, u_right),
        consts=(same, pick, fold, agree), down=down, up=up, g_down=g_down, g_up=g_up, live=live, mid=mid, n2=n2, act=act,
        dg=dg, acc=acc, gffn=gffn, put_res=put_res, gout=nrm, other=other,
    )
    third = Exchange(p, res, out, *sems[18:21])

    def norm(i):
        v = x[i].astype(jnp.float32)
        scale = lax.rsqrt(jnp.mean(v * v, axis=-1, keepdims=True) + NORM_EPS)
        nrm[rows_of(i, SEG), :] = (v * scale * gain[...]).astype(bf)

    def norms():
        first.finish()
        keep_x.start()
        each_of(x.shape[0], norm)
        keep_n.start()
        fill_mask(mask, lengths, p.m)
        fill_rows(rows, pos_table, onehot)
        layer.prepare(p.m)
        acc[...] = jnp.zeros_like(acc)

    def step(name):
        kind, rest = name[0], name[2:]
        if name == "n":
            norms()
        elif name in ("ex0", "ex1"):
            (first, second)[int(name[2])].start()
        elif kind == "s":
            arrays[rest].start()
        elif kind == "f":
            arrays[rest].finish()
        elif kind == "a":
            arrays[rest[0]].along(int(rest[1:]))
        elif kind == "c":
            arrays[rest[0]].across(int(rest[1:]))

    def steps(names):
        for name in names:
            step(name)

    plan = front_order()
    p.meet(0)
    steps(plan["first"])
    keep_q.start()

    def piece(m, place):
        at = sum(place) + place[0]
        for loop in range(4):
            names = plan.get(("A", 3 * loop + at))
            if names:
                pl.when(m == loop)(functools.partial(steps, names))

    def keeps(m):
        lanes = rows_of(m, D)
        return [
            pltpu.make_async_copy(packed.at[m], packed_hbm.at[m], local.at[3 + m]),
            pltpu.make_async_copy(act.at[:, lanes], long_hbm.at[m], local.at[7 + m]),
            pltpu.make_async_copy(dg.at[pl.ds(0, KEPT_REST), lanes], rest_hbm.at[m], local.at[11 + m]),
            pltpu.make_async_copy(ctx.at[m], ctx_hbm.at[m], local.at[15 + m]),
        ]

    def keep_probs(m, number, unit, h, probs):
        offset, length, q0, width = unit
        places = kept_at(offset, length, h)
        row, rows_kept, lane, _ = places[min(q0 // width, len(places) - 1)]
        lane = lane + (q0 if len(places) == 1 else 0)
        lanes = pl.ds(pl.multiple_of(D * m + lane, TILE), width)
        if row < KEPT_LONG:
            act[row : row + rows_kept, lanes] = probs
        else:
            dg[row - KEPT_LONG : row - KEPT_LONG + rows_kept, lanes] = probs

    def heads(m):
        w = gq[m // 2, m % 2].reshape(D, QKV_PAD)
        packed[m] = dot(nrm[...], w).astype(bf)
        keeps(m)[0].start()
        attend_group(
            packed.at[m], mask, rows[m], ctx.at[m], group, functools.partial(piece, m), functools.partial(keep_probs, m)
        )
        for copy in keeps(m)[1:]:
            copy.start()

    def stores(z):
        lanes = rows_of(z, chunk_rows)
        return [
            pltpu.make_async_copy(gi.at[z], gi_hbm.at[z], sem.at[0, z]),
            pltpu.make_async_copy(gu.at[z], gu_hbm.at[z], sem.at[1, z]),
            pltpu.make_async_copy(dg.at[:, lanes], dg_hbm.at[z], sem.at[2, z]),
        ]

    def weights(z):
        lanes = rows_of(z, chunk_rows)
        return pltpu.make_async_copy(act.at[pl.ds(0, chunk_rows), lanes], pu_hbm.at[z], sem.at[3, z])

    each_of(4, heads)
    steps(plan[("before", "O")])
    keep_o = pltpu.make_async_copy(go, go_hbm, out_sems.at[0])
    keep_o.start()
    each_of(layer.n // RCH, layer.midway)
    tail = [
        pltpu.make_async_copy(src, dst, out_sems.at[1 + k])
        for k, (src, dst) in enumerate(((mid, mid_hbm), (n2, n2_hbm), (nrm, gout_hbm), (gffn, gffn_hbm)))
    ]
    tail[0].start()
    tail[1].start()
    each_of(4, lambda m: [copy.wait() for copy in keeps(m)])

    def chunk(e):
        for k in range(depth):
            pl.when(e == k)(functools.partial(steps, plan[("before", f"F{k}")]))
        z = p.nearest(e)
        for name in "iu":
            arrays[name].finish_at(z)
        layer.forward(z)
        for copy in stores(z):
            copy.start()

    each_of(depth, chunk)
    second.finish()
    for copy in (keep_x, keep_n, keep_q):
        copy.wait()
    layer.adapter_all()
    third.start()
    tail[2].start()
    tail[3].start()

    def weights_out(k):
        z = p.order(k)
        lanes = rows_of(z, chunk_rows)
        act[:chunk_rows, lanes] = dot(act[:, lanes], gffn[...], TN).astype(bf)
        weights(z).start()

    for k in range(depth):
        weights_out(k)
    layer.adapter_grads()
    for copy in (keep_o, *tail):
        copy.wait()
    each_of(depth, lambda z: [copy.wait() for copy in (*stores(z), weights(z))])
    third.finish()
    for g in (*arrays.values(), first, second, third):
        g.drain()


def front(depth, group, tok, cot, shards, rows_of_shards, gains, lengths, pos_table, factors):
    hbm = pl.BlockSpec(memory_space=pl.ANY)
    vmem = pl.BlockSpec(memory_space=pltpu.VMEM)
    bf, f32 = jnp.bfloat16, jnp.float32
    shape = jax.ShapeDtypeStruct
    n = tok.shape[0] * SEG
    kept = [(rows, QKV_PAD if i == 0 else D) for i, rows in enumerate(rows_of_shards)]
    whole = [((2, 2, depth, 2) if i == 0 else (depth, 2, 2, 2)) + s for i, s in enumerate(kept)]
    ff = 8 * depth * kept[2][0]
    return pl.pallas_call(
        functools.partial(front_kernel, depth, group),
        out_shape=[
            shape(tok.shape, bf),
            shape(whole[0], bf),
            shape((n, D), bf),
            shape((4, n, QKV_PAD), bf),
            shape(tok.shape, bf),
            shape((n, D), f32),
            shape((4, n, CTX_PAD), bf),
            *[shape(s, bf) for s in whole[1:]],
            shape((depth, n, D), bf),
            shape((depth, D, D), bf),
            shape((n, D), bf),
            shape((n, D), bf),
            shape((n, D), bf),
            shape((4, KEPT_LONG, D), bf),
            shape((4, KEPT_REST, D), bf),
            shape((ROW_END, 128), f32),
        ],
        in_specs=[hbm] * 2 + [vmem] * 7 + [pl.BlockSpec(memory_space=pltpu.SMEM)] + [vmem] * 11,
        out_specs=[hbm] * 17 + [vmem],
        scratch_shapes=[pltpu.VMEM(s, bf) for s in kept]
        + [
            pltpu.VMEM((n, TILE), bf),
            pltpu.VMEM((4, 3, 512), f32),
            pltpu.VMEM(tok.shape, bf),
            pltpu.VMEM(tok.shape, bf),
            *[pltpu.VMEM(s, bf) for s in whole],
            pltpu.VMEM((n, D), bf),
            pltpu.VMEM((4, n, QKV_PAD), bf),
            pltpu.VMEM((4, n, CTX_PAD), bf),
            pltpu.VMEM((D, ADAPT_PAD), bf),
            pltpu.VMEM((D, ADAPT_PAD), bf),
            pltpu.VMEM((D, ADAPT_PAD), f32),
            pltpu.VMEM((D, ADAPT_PAD), f32),
            pltpu.VMEM((n, 1), f32),
            pltpu.VMEM((n, D), f32),
            pltpu.VMEM((n, D), bf),
            pltpu.VMEM((n, ff), bf),
            pltpu.VMEM((n, ff), bf),
            pltpu.VMEM((n, D), f32),
            pltpu.VMEM((n, D), bf),
            pltpu.VMEM(tok.shape, bf),
            pltpu.SemaphoreType.DMA((4, depth)),
            pltpu.SemaphoreType.DMA((5,)),
            pltpu.SemaphoreType.DMA((19,)),
        ]
        + Gather.sems(depth) * 4
        + Exchange.sems() * 3,
        compiler_params=pltpu.CompilerParams(
            collective_id=2, has_side_effects=True, vmem_limit_bytes=63 * 2**20
        ),
        name="front",
    )(
        tok, cot, *shards, jnp.asarray(column_choice(group), bf), *gains, lengths, pos_table,
        jnp.asarray(offset_onehot()), *factors, *map(jnp.asarray, adapter_constants()),
    )


BACK = (
    "Su2 Su0 Su3 Su1",
    "K K K Hu0",
    "K K Si0 Hu2",
    "K Si2 Hu3 Qu0",
    "K K K Si3",
    "Qu2 K So0 K",
    "So2 Si1 Hi0 K",
    "Qu3 K K Ho0",
    "K Fu3 Hi2 So3",
    "K K K K",
    "Hu1 Qo0 K Fu2",
    "K Ho2 Qi0 K",
    "K Ho3 Fu0 K",
    "K Hi3 K Qi2",
    "Hi1 Qu1 K So1",
    "K K Qo3 Fi0",
    "K K K Fo0",
    "Ho1 K Fu1 Qo2",
    "K Fo3 Qi3 Sq0",
    "N Fi3 Sq2 TB",
    "Hq0 Fi2 Sq3 T0",
    "Qi1 Qo1 Fi1 Hq2",
    "Fo1 Hq3 Qq0 Sq1",
    "Fo2 Cu Hq1 Qq2",
    "Fq0 T1 T2 Ci",
    "Eu x1 Qq3 Qq1",
    "Fq2 Fq1 Co Fq3",
    "Ei Cq T3 Eo",
    "Eq T4",
)


def back_order():
    plan, pieces = {}, 0
    for step in " ".join(BACK).split():
        if step in "KN":
            pieces += 1
        else:
            plan.setdefault(pieces, []).append(step)
    return plan


PIECES = 6


def back_kernel(
    depth, bits, group,
    tok_hbm, gq_hbm, nrm_hbm, packed_hbm, mid_hbm, ctx_hbm, go_hbm, gi_hbm, gu_hbm, dg_hbm, gffn_hbm, n2_hbm, gout_hbm,
    long_hbm, rest_hbm, pu, gain, gain_ffn, onehot, other,
    oq, oo, oi, ou, small, gtok,
    wu, wi, dg, acc, mid, gffn, nrm, gout, x, ctx, go, kept, g_gain, sums_s, mine_u, sem_u, local, chunk_sem, gq_sem, *scr,
):
    p = Place(depth)
    n = depth
    bf = jnp.bfloat16
    gain, gain_ffn = gain[...].reshape(1, D), gain_ffn[...].reshape(1, D)
    width = pl.ds(0, QKV_PAD)
    arrays = {
        "u": Scatter(p, False, pu, ou, *scr[0:6], mine_u, sem_u),
        "i": Scatter(p, False, wi, oi, *scr[6:12]),
        "o": Scatter(p, False, go, oo, *scr[12:18]),
        "q": Scatter(
            p, True, wu, oq, *scr[18:24],
            region=lambda core, z: wu.at[:, core, z // 2, z % 2, :, :, width],
        ),
    }
    row_g = Exchange(p, x, gtok, *scr[24:27])
    total = Sum(p, bits, small, *scr[27:30])
    layer = Layer(
        wo=lambda m: go[m].reshape(CTX_PAD, D), wi=lambda z: wi[z].reshape(-1, D),
        wu=lambda z: wu[z // 2, z % 2].reshape(-1, D), slope=lambda z: dg.at[z], ctx=ctx, gain=gain_ffn, g_gain=g_gain,
        mid=mid, n2=nrm, acc=acc, gffn=gffn, glow=gffn, gout=gout,
    )

    def load(src, dst, k):
        return pltpu.make_async_copy(src, dst, local.at[k])

    early = [
        load(src, dst, k)
        for k, (src, dst) in enumerate(
            ((gffn_hbm, gffn), (n2_hbm, nrm), (mid_hbm, mid), (gout_hbm, gout), (ctx_hbm, ctx), (go_hbm, go), (tok_hbm, x))
        )
    ]

    def chunk_in(k):
        z = p.order(k)
        pairs = ((dg_hbm.at[z], dg.at[z]), (gu_hbm.at[z], wu.at[z // 2, z % 2]), (gi_hbm.at[z], wi.at[z]))
        return [pltpu.make_async_copy(src, dst, chunk_sem.at[j, k]) for j, (src, dst) in enumerate(pairs)]

    def packed_in(m):
        return load(packed_hbm.at[m], dg.at[m, :, width], 8 + m)

    def gq_in(m, z):
        y, c = m // 2, m % 2
        return pltpu.make_async_copy(
            gq_hbm.at[y, c, z], wu.at[y, c, z // 2, z % 2, :, :, width], gq_sem.at[m, z]
        )

    def kept_in(m):
        slot = m % 2
        return [
            load(long_hbm.at[m], kept.at[slot, pl.ds(0, KEPT_LONG)], 12 + slot),
            load(rest_hbm.at[m], kept.at[slot, pl.ds(KEPT_LONG, KEPT_REST)], 14 + slot),
        ]

    todo = total.steps()

    def steps(names):
        for name in names:
            if name == "x1":
                row_g.start()
            elif name[0] == "T":
                todo.pop(0)()
            else:
                array = arrays[name[1]]
                if name[0] in "CE":
                    (array.collect if name[0] == "C" else array.finish)()
                else:
                    k = int(name[2:])
                    {"S": array.start, "H": array.to_half, "Q": array.to_quarter, "F": array.forward}[name[0]](k)
                    if name[0] == "Q":
                        array.origin(k)

    plan = back_order()

    def place(k):
        steps(plan.pop(k, ()))

    ahead_of = {1: chunk_in(2), 2: early[2:3], 3: chunk_in(3), 4: early[3:4], 5: early[4:6], 6: kept_in(0), 7: early[6:]}

    def load_ahead(k):
        for copy in ahead_of.get(k, ()):
            copy.start()

    p.greet(bits)
    for copy in (early[0], *chunk_in(0), early[1]):
        copy.start()
    small[...] = jnp.zeros_like(small)
    small[ROW_OTHER:, :] = other[...]
    acc[...] = jnp.zeros_like(acc)
    g_gain[...] = jnp.zeros_like(g_gain)
    p.meet(bits)
    place(0)
    for copy in chunk_in(1):
        copy.start()
    early[0].wait()
    for k in range(n):
        z = p.order(k)
        for copy in chunk_in(k):
            copy.wait()
        load_ahead(2 * k + 1)
        layer.backward(z)
        place(2 * k + 1)
        load_ahead(2 * k + 2)
        if k == 0:
            early[1].wait()
        wi[z] = dot(dg[z], nrm[...], TN).astype(bf).reshape(wi.shape[1:])
        place(2 * k + 2)
    for m in range(4):
        packed_in(m).start()
        for z in range(n):
            gq_in(m, z).start()
    renew = load(nrm_hbm, nrm, 7)
    renew.start()
    for copy in early[2:]:
        copy.wait()
    each_of(layer.n // RCH, layer.last)
    place(2 * n + 1)

    def project(m):
        go[m] = layer.projection(m).reshape(go.shape[1:])

    each_of(4, project)
    acc[...] = jnp.zeros_like(acc)
    place(2 * n + 2)
    renew.wait()
    for m in range(4):
        packed_in(m).wait()
        for z in range(n):
            gq_in(m, z).wait()

    def piece(m, j):
        for loop in range(4):
            names = plan.get(2 * n + 2 + PIECES * loop + j + 1)
            if names:
                pl.when(m == loop)(functools.partial(steps, names))

    def tick(m, at):
        number, head = at
        if number == 0:
            piece(m, head)
        elif head == 8:
            piece(m, 3)

    def heads(m):
        slot, y, c = m % 2, m // 2, m % 2
        for copy in kept_in(m):
            copy.wait()

        def ahead():
            for copy in kept_in(m + 1):
                copy.start()

        pl.when(m < 3)(ahead)
        packed = dg.at[m, :, width]
        attend_group_back(packed, Kept(kept.at[slot]), ctx.at[m], packed, sums_s.at[m], group, functools.partial(tick, m))
        whole = (Ellipsis, slice(0, QKV_PAD))
        acc[...] += dot(packed[...], wu[y, c][whole].reshape(D, QKV_PAD), NT)
        piece(m, 4)
        wu[y, c, :, :, :, :, 0:QKV_PAD] = dot(nrm[...], packed[...], TN).astype(bf).reshape(*wu.shape[2:6], QKV_PAD)
        piece(m, 5)

    each_of(4, heads)
    small[ROW_TABLE : ROW_TABLE + 16, :] = jnp.zeros((16, 128), jnp.float32)
    for m in range(4):
        small[ROW_TABLE + 3 * m : ROW_TABLE + 3 * m + 3, :] = precise(sums_s[m], onehot[...])
    put_row(small, ROW_OTHER + ROW_FFN, g_gain[...])

    def last(s, g_gain):
        r = rows_of(s, SEG)
        v = x[s].astype(jnp.float32)
        g_n1 = acc[r, :]
        scale = lax.rsqrt(jnp.mean(v * v, axis=-1, keepdims=True) + NORM_EPS)
        scaled = gain * g_n1
        centre = jnp.mean(v * scaled, axis=-1, keepdims=True)
        x[s] = (mid[r, :] + scale * scaled - v * (scale * scale * scale * centre)).astype(bf)
        return g_gain + jnp.sum(v * scale * g_n1, axis=0, keepdims=True)

    put_row(small, ROW_GAIN, lax.fori_loop(0, x.shape[0], last, jnp.zeros((1, D), jnp.float32)))
    place(2 * n + 2 + 4 * PIECES + 1)
    row_g.finish()
    for g in (*arrays.values(), row_g, total):
        g.drain()


def back(depth, bits, group, kept, ffn, pu, gains, onehot, other):
    hbm = pl.BlockSpec(memory_space=pl.ANY)
    vmem = pl.BlockSpec(memory_space=pltpu.VMEM)
    bf, f32 = jnp.bfloat16, jnp.float32
    shape = jax.ShapeDtypeStruct
    tok, gq = kept[:2]
    mid, ctx, go, gi = ffn[:4]
    n = mid.shape[0]
    small_rows = ROW_OTHER + other.shape[0]
    outs = [shape(s.shape[4:], f32) for s in (gq, go, gi, gi)]
    outs += [shape((small_rows, 128), f32), shape(tok.shape, bf)]
    dma = pltpu.SemaphoreType.DMA
    scratch = [
        pltpu.VMEM((2, 2, 2, 2, 2, *gi.shape[4:]), bf),
        pltpu.VMEM(gi.shape, bf),
        pltpu.VMEM((depth, n, D), bf),
        pltpu.VMEM((n, D), f32),
        pltpu.VMEM((n, D), f32),
        pltpu.VMEM((n, D), bf),
        pltpu.VMEM((n, D), bf),
        pltpu.VMEM((n, D), bf),
        pltpu.VMEM(tok.shape, bf),
        pltpu.VMEM(ctx.shape, bf),
        pltpu.VMEM(go.shape, bf),
        pltpu.VMEM((2, KEPT_LONG + KEPT_REST, D), bf),
        pltpu.VMEM((1, D), f32),
        pltpu.VMEM((4, 3, 768), f32),
        pltpu.VMEM((depth, 2, 2) + gi.shape[4:], bf),
        dma((depth,)),
        dma((16,)),
        dma((3, depth)),
        dma((4, depth)),
    ]
    for s in (gi, gi, go, gq):
        scratch += Scatter.scratch(depth, *s.shape[4:])
    scratch += Exchange.sems() + Sum.scratch(bits, small_rows)
    return pl.pallas_call(
        functools.partial(back_kernel, depth, bits, group),
        out_shape=outs,
        in_specs=[hbm] * 16 + [vmem] * 4,
        out_specs=[vmem] * 5 + [hbm],
        scratch_shapes=scratch,
        compiler_params=pltpu.CompilerParams(
            collective_id=3, has_side_effects=True, vmem_limit_bytes=63 * 2**20
        ),
        name="back",
    )(*kept, *ffn, pu.reshape(gi.shape), *gains, onehot, other)


def finish_kernel(
    q, o, i, u, small, choice,
    gq, go, gi, gu, g_attn, g_ffn, g_table, g_rules, g_dl, g_dr, g_ul, g_ur,
):
    left = q[: gq.shape[1], :]
    parts = []
    for _ in range(3):
        parts.append(left.astype(jnp.bfloat16))
        left = left - parts[-1].astype(jnp.float32)
    for h in range(3):
        chosen = choice[3 * DH * h : 3 * DH * (h + 1), :]
        gq[h] = sum(dot(part, chosen, NT) for part in parts)
    go[...] = o[: go.shape[0], :]
    gi[...] = i[: gi.shape[0], :]
    gu[...] = u[: gu.shape[0], :]
    for k in range(D // 128):
        lanes = slice(128 * k, 128 * (k + 1))
        g_attn[lanes] = small[ROW_GAIN + k, :]
        g_ffn[lanes] = small[ROW_OTHER + ROW_FFN + k, :]
    g_table[...] = small[ROW_TABLE : ROW_TABLE + g_table.shape[0], :NB]
    for i in range(KRON):
        at = ROW_OTHER + ROW_RULES + 4 * i
        g_rules[i] = small[at : at + 4, :KRON]
    for ref, at in ((g_dl, ROW_OTHER + ROW_DL), (g_ur, ROW_OTHER + ROW_UR)):
        ref[:, :128] = small[at : at + 4, :]
        ref[:, 128:] = small[at + 4 : at + 8, : ref.shape[1] - 128]
    for ref, at in ((g_dr, ROW_OTHER + ROW_DR), (g_ul, ROW_OTHER + ROW_UL)):
        ref[...] = small[at : at + 4, :KA]


def finish(q, o, i, u, small, group, shapes):
    vmem = pl.BlockSpec(memory_space=pltpu.VMEM)
    return pl.pallas_call(
        finish_kernel,
        out_shape=[jax.ShapeDtypeStruct(s, jnp.float32) for s in shapes],
        in_specs=[vmem] * 6,
        out_specs=[vmem] * 12,
        name="finish",
    )(q, o, i, u, small, jnp.asarray(column_choice(group), jnp.bfloat16))


def round_up(n, m):
    return -(-n // m) * m


def pad_rows(a, rows):
    return jnp.pad(a, ((0, rows - a.shape[0]), (0, 0)))


HEADS = 12


def local(
    tokens,
    lengths,
    cotangent,
    w_qkv,
    w_o,
    w_in,
    w_out,
    gain_attn,
    gain_ffn,
    pos_table,
    phm_rules,
    down_left,
    down_right,
    up_left,
    up_right,
):
    dp_count, mp_count = lax.axis_size("dp"), lax.axis_size("mp")
    depth = dp_count // 2
    bits = dp_count.bit_length() - 1
    devices = dp_count * mp_count
    member = lax.axis_index("mp")
    tok_rows = tokens.shape[0]
    seg_count = tok_rows // SEG
    o_rows, in_rows, q_rows = w_o.shape[0], w_in.shape[1], w_qkv.shape[0]
    bf = jnp.bfloat16
    group = o_rows if o_rows % 24 == 0 and round_up(o_rows, 16) * 3 == o_rows * 4 else 3 * DH
    rows_of_shards = [round_up(r, 16) for r in (q_rows, o_rows, in_rows, in_rows)]
    tok_in, cot_in = tokens.reshape(seg_count, SEG, D), cotangent.reshape(seg_count, SEG, D)
    merged = depth == 4 and group == o_rows and rows_of_shards[0] == q_rows and rows_of_shards[2] == in_rows
    factors = (phm_rules, down_left, down_right, up_left, up_right)
    gains = (gain_attn, gain_ffn)
    if merged:
        shards = (w_qkv.transpose(1, 0, 2), w_o, w_in.T, w_out)
        *kept, out, mid, ctx, go, gi, gu, dg, pu, gffn, n2, gout, long, rest, other = front(
            depth, group, tok_in, cot_in, shards, rows_of_shards, gains, lengths, pos_table.T, factors
        )
    else:
        shards = (head_columns(w_qkv.astype(bf), group), w_o.astype(bf), w_in.astype(bf).T, w_out.astype(bf))
        shards = [pad_rows(s, r) for s, r in zip(shards, rows_of_shards)]
        tok_s, cot_s, gq, go, gi, gu = gather_all(depth, tok_in, cot_in, shards)
    def plain(g, rows):
        return g.reshape(devices, g.shape[-2], D)[:, :rows].reshape(devices * rows, D)

    def slots(g, rows):
        padded = jnp.pad(g.reshape(devices, rows, D), ((0, 0), (0, round_up(rows, 16) - rows), (0, 0)))
        return padded.reshape(depth, 2, 2, 2, padded.shape[1], D)

    if not merged:
        tokens_s = tok_s.reshape(tok_rows, D)
        if group == o_rows:
            dense_o = go.reshape(mp_count, CTX_PAD, D)
        else:
            dense_o = plain(go, o_rows).reshape(mp_count, 3 * DH, D)
            dense_o = jnp.pad(dense_o, ((0, 0), (0, CTX_PAD - 3 * DH), (0, 0)))
        qkv_full = gq.reshape(mp_count, dp_count, rows_of_shards[0], QKV_PAD)[:, :, :q_rows]
        qkv_full = qkv_full.reshape(mp_count, D, QKV_PAD)
        live = jnp.concatenate(
            [jnp.arange(length) < own_length(lengths, member, i) for i, (_, length) in enumerate(SPANS)]
        )
        mask = key_mask(live)
        rows = jnp.einsum("bh,br->hr", pos_table, offset_onehot(), precision=FULL_PRECISION).reshape(mp_count, 3, 512)
        normed_attn, packed, context = attention(tokens_s, gains[0].reshape(1, D), qkv_full, mask, rows, group)
        result, grad_mid, grad_context, grad_w_o, grad_w_in, grad_w_out, other = middle(
            tokens_s,
            context,
            dense_o,
            plain(gi, in_rows),
            plain(gu, in_rows),
            cot_s.reshape(tok_rows, D),
            gains[1],
            lengths,
            factors,
        )
    onehot = jnp.asarray(np.pad(table_onehot(), ((0, 0), (0, 128 - NB))))
    if merged:
        oq, oo, oi, ou, summed, gtok = back(
            depth, bits, group, kept, (mid, ctx, go, gi, gu, dg, gffn, n2, gout, long, rest), pu, gains, onehot, other
        )
    else:
        if group == o_rows:
            part_o = grad_w_o.reshape(depth, 2, 2, 2, round_up(o_rows, 16), D)
        else:
            part_o = slots(grad_w_o.reshape(mp_count, CTX_PAD, D)[:, : 3 * DH].reshape(D, D), o_rows)
        result = result.reshape(seg_count, SEG, D)
        packed_grads, sums = attention_back(packed, grad_context, mask, rows, group)
        table_grad = jnp.dot(sums.reshape(HEADS, 768), onehot, precision=FULL_PRECISION)
        grad_w_qkv = jnp.einsum("td,mtc->mdc", normed_attn, packed_grads, preferred_element_type=jnp.float32).astype(bf)
        grad_n1 = jnp.einsum("mtc,mdc->td", packed_grads, qkv_full, preferred_element_type=jnp.float32)
        _, norm_back_attn = jax.vjp(normed, tokens_s.astype(jnp.float32), gain_attn)
        grad_x_part, grad_gain_attn = norm_back_attn(grad_n1)
        grad_tokens = (grad_mid + grad_x_part).astype(bf)
        small = jnp.concatenate([
            jnp.pad(grad_gain_attn.reshape(D // 128, 128), ((0, ROW_TABLE - D // 128), (0, 0))),
            jnp.pad(table_grad, ((0, ROW_OTHER - ROW_TABLE - HEADS), (0, 0))),
            other,
        ])
        part_q = grad_w_qkv.reshape(mp_count, dp_count, q_rows, QKV_PAD)
        part_q = jnp.pad(part_q, ((0, 0), (0, 0), (0, rows_of_shards[0] - q_rows), (0, 0)))
        part_q = part_q.reshape(2, 2, depth, 2, rows_of_shards[0], QKV_PAD)
        oq, oo, oi, ou, summed, out, gtok = scatter_all(
            depth, bits, (part_q, part_o, slots(grad_w_in, in_rows), slots(grad_w_out, in_rows)), small, result, grad_tokens.reshape(seg_count, SEG, D)
        )
    shapes = (
        (3, q_rows, 3 * DH), w_o.shape, w_in.shape[::-1], w_out.shape, (D,), (D,), pos_table.shape[::-1],
        phm_rules.shape, down_left.shape, down_right.shape, up_left.shape, up_right.shape,
    )
    g_qkv, g_o, g_in, g_out, g_attn, g_ffn, g_table, *smalls = finish(oq, oo, oi, ou, summed, group, shapes)
    return (
        out.reshape(tok_rows, D),
        gtok.reshape(tok_rows, D),
        g_qkv.transpose(1, 0, 2),
        g_o,
        g_in.T,
        g_out,
        g_attn,
        g_ffn,
        g_table.T,
        *smalls,
    )


def solution(mesh):
    return jax.shard_map(
        local,
        mesh=mesh,
        in_specs=(
            P(("dp", "mp"), None),
            P("dp"),
            P(("dp", "mp"), None),
            P("dp", "mp", None),
            P(("dp", "mp"), None),
            P(None, ("dp", "mp")),
            P(("dp", "mp"), None),
            P(),
            P(),
            P(),
            P(),
            P(),
            P(),
            P(),
            P(),
        ),
        out_specs=(
            P(("dp", "mp"), None),
            P(("dp", "mp"), None),
            P("dp", "mp", None),
            P(("dp", "mp"), None),
            P(None, ("dp", "mp")),
            P(("dp", "mp"), None),
            P(),
            P(),
            P(),
            P(),
            P(),
            P(),
            P(),
            P(),
        ),
        check_vma=False,
    )
```

profile of v0, /device:TPU:0, one launch (start us, length us, event | category | flops | bytes accessed | tf_op | source)
XLA Modules:
  0.0 209.0 jit_solution(875335367650732739)
XLA Ops:
  0.7 101.4 %front.1 = (bf16[8,128,768]{2,1,0:T(8,128)(2,1)}, bf16[2,2,4,2,96,640]{5,4,3,2,1,0:T(8,128)(2,1)}, bf16[1024,768]{1,0:T(8,128)(2,1)}, bf16[4,1024,640]{2,1,0:T(8...) custom-call(bf16[8,128,768]{2,1,0:T(8,128)(2,1)} %bitcast.14, ...), custom_call_target="tpu_custom_call" | custom-call | tf_op jit(solution)/shard_map/front/pallas_call | solution.py:1521
  102.1 100.2 %back.1 = (f32[96,640]{1,0:T(8,128)}, f32[32,768]{1,0:T(8,128)}, f32[96,768]{1,0:T(8,128)}, f32[96,768]{1,0:T(8,128)}, f32[72,128]{1,0:T(8,128)}, /*index=5*/bf16[8,128,768]{2,1,0:T(8,128)(2,1)}) custom-call(bf16[8,128,768]{2,1,0:T(8,128)(2,1)} %get-tuple-element.51.tok_hbm, bf16[2,2,4,2,96,640]{5,4,3,2,1,0:T(8,128)(2,1)} %get-tuple-element.52.gq_hbm, ...), custom_call_target="tpu_custom_call" | custom-call | tf_op jit(solution)/shard_map/back/pallas_call | solution.py:1853
  202.3 0.0 copy-start
  202.3 3.4 %finish.1 = (f32[3,96,192]{2,1,0:T(8,128)}, f32[24,768]{1,0:T(8,128)}, f32[96,768]{1,0:T(8,128)}, f32[96,768]{1,0:T(8,128)}, f32[768]{0:T(1024)}, /*index=5*/f32...) custom-call(f32[96,640]{1,0:T(8,128)} %get-tuple-element.69.q, ...), custom_call_target="tpu_custom_call" | custom-call | tf_op jit(solution)/shard_map/finish/pallas_call | solution.py:1898
  205.7 0.0 copy-done
  205.7 0.0 copy-start.1
  205.7 1.1 copy.39
  206.9 0.8 copy-done.1
  207.7 1.1 copy.40
Async XLA Ops:
  202.3 3.4 %copy-start = (bf16[8,128,768]{2,1,0:T(8,128)(2,1)S(1)}, bf16[8,128,768]{2,1,0:T(8,128)(2,1)}, u32[]{:S(2)}) copy-start(bf16[8,128,768]{2,1,0:T(8,128)(2,1)} %get-tuple-element.50) | copy-start | bytes 4718596
  205.7 2.0 copy-start.1
where the time goes:
time: 212 us; the launch traced here: 209 us
  Pallas kernels  205 us (97%)
  local copies, waits for them, and re-layouts  3.11 us (1%)
    pallas_call x1, Pallas kernels, front(): pl.pallas_call(functools.partial(front_kernel, depth, group), out_shape=[...  101 us
    pallas_call x1, Pallas kernels, back(): pl.pallas_call(functools.partial(back_kernel, depth, bits, group), out_sh...  100 us

commit v1 on v0

--- a/solution.py
+++ b/solution.py
@@ -972,15 +972,11 @@
     return (np.arange(NB)[:, None] == buckets[offset][None, :]).astype(np.float32)
 
 
-def column_choice(group):
-    choice = np.zeros((9 * DH, QKV_PAD), np.float32)
-    for h in range(3):
-        for k in range(2 * DH):
-            choice[3 * DH * h + k, TILE * h + k] = 1
+def value_choice(group):
+    choice = np.zeros((3 * DH, CTX_PAD), np.float32)
     heads, column = value_lanes(group)
-    for lane in range(CTX_PAD):
-        if heads[lane] >= 0:
-            choice[3 * DH * heads[lane] + 2 * DH + column[lane] % DH, 3 * TILE + lane] = 1
+    lanes = np.flatnonzero(heads >= 0)
+    choice[column[lanes], lanes] = 1
     return choice
 
 
@@ -1340,8 +1336,10 @@
     bf = jnp.bfloat16
     p.greet(0)
     gain, gain_ffn = gain[...].reshape(1, D), gain_ffn[...].reshape(1, D)
-    per_head = [dot(w_qkv[h].astype(bf), choice[3 * DH * h : 3 * DH * (h + 1), :]) for h in range(3)]
-    wq[...] = sum(per_head).astype(bf)
+    for h in range(3):
+        wq[:, TILE * h : TILE * (h + 1)] = w_qkv[h, :, :TILE].astype(bf)
+    values = [dot(w_qkv[h, :, TILE:].astype(bf), choice[DH * h : DH * (h + 1), :]) for h in range(3)]
+    wq[:, 3 * TILE :] = sum(values).astype(bf)
     wo[...] = jnp.zeros_like(wo)
     wo[: w_o.shape[0], :] = w_o[...].astype(bf)
     wi[...] = w_in[...].astype(bf)
@@ -1573,41 +1571,41 @@
         ),
         name="front",
     )(
-        tok, cot, *shards, jnp.asarray(column_choice(group), bf), *gains, lengths, pos_table,
+        tok, cot, *shards, jnp.asarray(value_choice(group), bf), *gains, lengths, pos_table,
         jnp.asarray(offset_onehot()), *factors, *map(jnp.asarray, adapter_constants()),
     )
 
 
 BACK = (
-    "Su2 Su0 Su3 Su1",
-    "K K K Hu0",
-    "K K Si0 Hu2",
-    "K Si2 Hu3 Qu0",
-    "K K K Si3",
-    "Qu2 K So0 K",
-    "So2 Si1 Hi0 K",
-    "Qu3 K K Ho0",
-    "K Fu3 Hi2 So3",
+    "Su0 Su2 K Su3",
+    "K Hu0 Si0 K",
+    "Hu2 K Hu3 K",
+    "K Qu0 Su1 K",
+    "Si2 Qu2 K K",
+    "Hi0 K So0 So1",
+    "K So2 Si1 K",
+    "Qu3 K K K",
+    "Hu1 So3 K K",
+    "Si3 Ho2 K K",
+    "Fu0 Qi0 Ho0 Hi1",
+    "K K Hi2 K",
+    "Qo2 K K K",
+    "K Qu1 K Fu2",
+    "Qo0 K K Qi2",
+    "Hi3 K Fu1 Fi0",
     "K K K K",
-    "Hu1 Qo0 K Fu2",
-    "K Ho2 Qi0 K",
-    "K Ho3 Fu0 K",
-    "K Hi3 K Qi2",
-    "Hi1 Qu1 K So1",
-    "K K Qo3 Fi0",
-    "K K K Fo0",
-    "Ho1 K Fu1 Qo2",
-    "K Fo3 Qi3 Sq0",
-    "N Fi3 Sq2 TB",
-    "Hq0 Fi2 Sq3 T0",
-    "Qi1 Qo1 Fi1 Hq2",
-    "Fo1 Hq3 Qq0 Sq1",
-    "Fo2 Cu Hq1 Qq2",
-    "Fq0 T1 T2 Ci",
-    "Eu x1 Qq3 Qq1",
-    "Fq2 Fq1 Co Fq3",
-    "Ei Cq T3 Eo",
-    "Eq T4",
+    "Sq0 Qi3 Fi3 Sq2",
+    "Sq3 Ho1 Ho3 Fo0",
+    "Hq0 Qi1 N Fu3",
+    "Qo3 Fi2 Qo1 TB",
+    "Sq1 Fo2 Hq2 Cu",
+    "Qq0 Fo1 T0 Hq1",
+    "Eu Hq3 Fi1 Fo3",
+    "T1 Co Qq2 Qq1",
+    "x1 Fq0 T2 Qq3",
+    "Eo Ci Fq2 Fq3",
+    "Fq1 Ei Cq T3",
+    "T4 Eq",
 )
 
 
@@ -1864,17 +1862,25 @@
 
 
 def finish_kernel(
-    q, o, i, u, small, choice,
-    gq, go, gi, gu, g_attn, g_ffn, g_table, g_rules, g_dl, g_dr, g_ul, g_ur,
+    q, o, i, u, small, choice, out_hbm, gtok_hbm,
+    gq, go, gi, gu, g_attn, g_ffn, g_table, g_rules, g_dl, g_dr, g_ul, g_ur, out, gtok, held, sems,
 ):
-    left = q[: gq.shape[1], :]
+    rows_in = [pltpu.make_async_copy(src, held.at[k], sems.at[k]) for k, src in enumerate((out_hbm, gtok_hbm))]
+    rows_out = [pltpu.make_async_copy(held.at[k], dst, sems.at[2 + k]) for k, dst in enumerate((out, gtok))]
+    for copy in rows_in:
+        copy.start()
+    left = q[: gq.shape[1], 3 * TILE :]
     parts = []
     for _ in range(3):
         parts.append(left.astype(jnp.bfloat16))
         left = left - parts[-1].astype(jnp.float32)
     for h in range(3):
-        chosen = choice[3 * DH * h : 3 * DH * (h + 1), :]
-        gq[h] = sum(dot(part, chosen, NT) for part in parts)
+        gq[h, :, :TILE] = q[: gq.shape[1], TILE * h : TILE * (h + 1)]
+        chosen = choice[DH * h : DH * (h + 1), :]
+        gq[h, :, TILE:] = sum(dot(part, chosen, NT) for part in parts)
+    for copy_in, copy_out in zip(rows_in, rows_out):
+        copy_in.wait()
+        copy_out.start()
     go[...] = o[: go.shape[0], :]
     gi[...] = i[: gi.shape[0], :]
     gu[...] = u[: gu.shape[0], :]
@@ -1891,17 +1897,23 @@
         ref[:, 128:] = small[at + 4 : at + 8, : ref.shape[1] - 128]
     for ref, at in ((g_dr, ROW_OTHER + ROW_DR), (g_ul, ROW_OTHER + ROW_UL)):
         ref[...] = small[at : at + 4, :KA]
-
-
-def finish(q, o, i, u, small, group, shapes):
+    for copy in rows_out:
+        copy.wait()
+
+
+def finish(q, o, i, u, small, out, gtok, group, shapes):
     vmem = pl.BlockSpec(memory_space=pltpu.VMEM)
+    hbm = pl.BlockSpec(memory_space=pl.ANY)
     return pl.pallas_call(
         finish_kernel,
-        out_shape=[jax.ShapeDtypeStruct(s, jnp.float32) for s in shapes],
-        in_specs=[vmem] * 6,
-        out_specs=[vmem] * 12,
+        out_shape=[jax.ShapeDtypeStruct(s, jnp.float32) for s in shapes]
+        + [jax.ShapeDtypeStruct(a.shape, a.dtype) for a in (out, gtok)],
+        in_specs=[vmem] * 6 + [hbm] * 2,
+        out_specs=[vmem] * 12 + [hbm] * 2,
+        scratch_shapes=[pltpu.VMEM((2, *out.shape), out.dtype), pltpu.SemaphoreType.DMA((4,))],
+        compiler_params=pltpu.CompilerParams(vmem_limit_bytes=60 * 2**20),
         name="finish",
-    )(q, o, i, u, small, jnp.asarray(column_choice(group), jnp.bfloat16))
+    )(q, o, i, u, small, jnp.asarray(value_choice(group), jnp.bfloat16), out, gtok)
 
 
 def round_up(n, m):
@@ -2022,7 +2034,9 @@
         (3, q_rows, 3 * DH), w_o.shape, w_in.shape[::-1], w_out.shape, (D,), (D,), pos_table.shape[::-1],
         phm_rules.shape, down_left.shape, down_right.shape, up_left.shape, up_right.shape,
     )
-    g_qkv, g_o, g_in, g_out, g_attn, g_ffn, g_table, *smalls = finish(oq, oo, oi, ou, summed, group, shapes)
+    g_qkv, g_o, g_in, g_out, g_attn, g_ffn, g_table, *smalls, out, gtok = finish(
+        oq, oo, oi, ou, summed, out, gtok, group, shapes
+    )
     return (
         out.reshape(tok_rows, D),
         gtok.reshape(tok_rows, D),

time: 212 us -> 209 us (0.986)
  local copies, waits for them, and re-layouts: 3.11 us -> 0 us
    unnamed x6 -> x0, local copies, waits for them, and re-layouts: 3.11 us -> none
where the time goes in v1:
time: 209 us; the launch traced here: 206 us
  Pallas kernels  205 us (98%)
    pallas_call x1, Pallas kernels, front(): pl.pallas_call(functools.partial(front_kernel, depth, group), out_shape=[...  101 us
    pallas_call x1, Pallas kernels, back(): pl.pallas_call(functools.partial(back_kernel, depth, bits, group), out_sh...  98.9 us
    pallas_call x1, Pallas kernels, finish(): pl.pallas_call(finish_kernel, out_shape=[jax.ShapeDtypeStruct(s, jnp.floa...  5.33 us

profile of v1, /device:TPU:0, one launch (start us, length us, event | category | flops | bytes accessed | tf_op | source)
XLA Modules:
  0.0 206.3 jit_solution(12173834330931563278)
XLA Ops:
  0.7 101.2 %front.1 = (bf16[8,128,768]{2,1,0:T(8,128)(2,1)}, bf16[2,2,4,2,96,640]{5,4,3,2,1,0:T(8,128)(2,1)}, bf16[1024,768]{1,0:T(8,128)(2,1)}, bf16[4,1024,640]{2,1,0:T(8...) custom-call(bf16[8,128,768]{2,1,0:T(8,128)(2,1)} %bitcast.12, ...), custom_call_target="tpu_custom_call" | custom-call | tf_op jit(solution)/shard_map/front/pallas_call | solution.py:1519
  101.8 98.9 %back.1 = (f32[96,640]{1,0:T(8,128)}, f32[32,768]{1,0:T(8,128)}, f32[96,768]{1,0:T(8,128)}, f32[96,768]{1,0:T(8,128)}, f32[72,128]{1,0:T(8,128)}, /*index=5*/bf16[8,128,768]{2,1,0:T(8,128)(2,1)}) custom-call(bf16[8,128,768]{2,1,0:T(8,128)(2,1)} %get-tuple-element.52.tok_hbm, bf16[2,2,4,2,96,640]{5,4,3,2,1,0:T(8,128)(2,1)} %get-tuple-element.53.gq_hbm, ...), custom_call_target="tpu_custom_call" | custom-call | tf_op jit(solution)/shard_map/back/pallas_call | solution.py:1851
  200.8 5.3 %finish.1 = (f32[3,96,192]{2,1,0:T(8,128)}, f32[24,768]{1,0:T(8,128)}, f32[96,768]{1,0:T(8,128)}, f32[96,768]{1,0:T(8,128)}, f32[768]{0:T(1024)}, /*index=5*/f32...) custom-call(f32[96,640]{1,0:T(8,128)} %get-tuple-element.69.q, ...), custom_call_target="tpu_custom_call" | custom-call | tf_op jit(solution)/shard_map/finish/pallas_call | solution.py:1907

commit v2 on v1

--- a/solution.py
+++ b/solution.py
@@ -1577,35 +1577,35 @@
 
 
 BACK = (
-    "Su0 Su2 K Su3",
-    "K Hu0 Si0 K",
-    "Hu2 K Hu3 K",
-    "K Qu0 Su1 K",
-    "Si2 Qu2 K K",
-    "Hi0 K So0 So1",
-    "K So2 Si1 K",
-    "Qu3 K K K",
-    "Hu1 So3 K K",
-    "Si3 Ho2 K K",
-    "Fu0 Qi0 Ho0 Hi1",
-    "K K Hi2 K",
-    "Qo2 K K K",
-    "K Qu1 K Fu2",
-    "Qo0 K K Qi2",
-    "Hi3 K Fu1 Fi0",
-    "K K K K",
-    "Sq0 Qi3 Fi3 Sq2",
-    "Sq3 Ho1 Ho3 Fo0",
-    "Hq0 Qi1 N Fu3",
-    "Qo3 Fi2 Qo1 TB",
-    "Sq1 Fo2 Hq2 Cu",
-    "Qq0 Fo1 T0 Hq1",
-    "Eu Hq3 Fi1 Fo3",
+    "Su2 Su0 K Su3",
+    "K Hu0 K Hu2",
+    "K K Hu3 Si0",
+    "Su1 K Qu0 K",
+    "Qu2 K K Si2",
+    "Hi0 K So3 So0",
+    "So2 K Hu1 K",
+    "Qu3 K K Ho2",
+    "K Ho3 Qi0 Si3",
+    "Ho0 Fu0 K K",
+    "K K Qu1 Si1",
+    "Qo2 K Hi2 K",
+    "K K Qo0 K",
+    "K K Fu2 Hi1",
+    "Fu1 K K Qi2",
+    "K Hi3 K So1",
+    "K K Fi0 K",
+    "K Sq0 Qi3 Sq2",
+    "Sq3 Fo0 Ho1 Hq0",
+    "Qo3 Fi2 N Fu3",
+    "Fo2 Hq2 TB Fi3",
+    "Cu Qi1 Qo1 Sq1",
+    "Fo3 Qq0 Fo1 T0",
+    "Hq1 Eu Hq3 Fi1",
     "T1 Co Qq2 Qq1",
-    "x1 Fq0 T2 Qq3",
-    "Eo Ci Fq2 Fq3",
-    "Fq1 Ei Cq T3",
-    "T4 Eq",
+    "Fq0 Eo x1 T2",
+    "Fq2 Fq1 Qq3 Ci",
+    "T3 Fq3 Cq T4",
+    "Ei Eq",
 )
 
 

time: 209 us -> 211 us (level)
  no operation moved by 1% of the time
where the time goes in v2:
time: 211 us; the launch traced here: 208 us
  Pallas kernels  207 us (98%)
    pallas_call x1, Pallas kernels, front(): pl.pallas_call(functools.partial(front_kernel, depth, group), out_shape=[...  101 us
    pallas_call x1, Pallas kernels, back(): pl.pallas_call(functools.partial(back_kernel, depth, bits, group), out_sh...  100 us
    pallas_call x1, Pallas kernels, finish(): pl.pallas_call(finish_kernel, out_shape=[jax.ShapeDtypeStruct(s, jnp.floa...  5.33 us

profile of v2, /device:TPU:0, one launch (start us, length us, event | category | flops | bytes accessed | tf_op | source)
XLA Modules:
  0.0 207.6 jit_solution(7991928300719000558)
XLA Ops:
  0.7 101.2 %front.1 = (bf16[8,128,768]{2,1,0:T(8,128)(2,1)}, bf16[2,2,4,2,96,640]{5,4,3,2,1,0:T(8,128)(2,1)}, bf16[1024,768]{1,0:T(8,128)(2,1)}, bf16[4,1024,640]{2,1,0:T(8...) custom-call(bf16[8,128,768]{2,1,0:T(8,128)(2,1)} %bitcast.12, ...), custom_call_target="tpu_custom_call" | custom-call | tf_op jit(solution)/shard_map/front/pallas_call | solution.py:1519
  101.8 100.3 %back.1 = (f32[96,640]{1,0:T(8,128)}, f32[32,768]{1,0:T(8,128)}, f32[96,768]{1,0:T(8,128)}, f32[96,768]{1,0:T(8,128)}, f32[72,128]{1,0:T(8,128)}, /*index=5*/bf16[8,128,768]{2,1,0:T(8,128)(2,1)}) custom-call(bf16[8,128,768]{2,1,0:T(8,128)(2,1)} %get-tuple-element.52.tok_hbm, bf16[2,2,4,2,96,640]{5,4,3,2,1,0:T(8,128)(2,1)} %get-tuple-element.53.gq_hbm, ...), custom_call_target="tpu_custom_call" | custom-call | tf_op jit(solution)/shard_map/back/pallas_call | solution.py:1851
  202.1 5.3 %finish.1 = (f32[3,96,192]{2,1,0:T(8,128)}, f32[24,768]{1,0:T(8,128)}, f32[96,768]{1,0:T(8,128)}, f32[96,768]{1,0:T(8,128)}, f32[768]{0:T(1024)}, /*index=5*/f32...) custom-call(f32[96,640]{1,0:T(8,128)} %get-tuple-element.69.q, ...), custom_call_target="tpu_custom_call" | custom-call | tf_op jit(solution)/shard_map/finish/pallas_call | solution.py:1907
